TPU v7x, 32 devices: a whole 2x2x4 slice. The times are simulated.
32 devices in a mesh: slab: 4 (over y, x), tile: 8 (over z, core).
Axes of the slice: x: 2, y: 2, z: 4, core: 2. Of those that a mesh axis runs over, the one named last changes fastest.
Arguments:
- particles: float32 [7, 8, 16, 1536], P(None, 'slab', 'tile')
- counts: int32 [8, 16, 48], P('slab', 'tile'), may hold values from 10 to 32, as said below
- leavers: int32 [2, 4, 16, 48], P(None, 'slab', 'tile'), may hold values from 0 to 4, as said below
Outputs:
- kept: float32 [7, 8, 16, 1536], P(None, 'slab', 'tile')
- arrivals: float32 [2, 7, 6144], P(None, None, ('slab', 'tile'))
Inputs may be any that keep to these rules, and one draw needn't show every extreme that they name: `counts`: one cell holds exactly 32. Over the 2 x 48 cells of one face of one device the leavers sum to exactly 192; one face cell of each face has 4.
All inputs are finite; a program needn't handle non-finite values.
Results may differ from a plain program's by a relative error of at most 0.0003.
Values sent between devices are 32-bit elements; how exact they have to be, the bound alone decides.
A program may use at most 128 MiB of HBM per device.

v0:
```python
import math

import jax
import jax.numpy as jnp
from jax import lax
from jax.sharding import PartitionSpec as P

SLOTS = 32
LMAX = 4


sound_speed = 10.0
smoothing = 0.5
cell_side = 2.0 * smoothing
kernel_norm = 21.0 / (16.0 * math.pi * smoothing**3)
grad_scale = -5.0 * kernel_norm / (smoothing * smoothing)
eos_stiff = sound_speed * sound_speed / 7.0
particle_mass = 0.125
viscosity = 0.1
visc_floor = 0.01 * smoothing * smoothing
time_step = 0.01
gravity = 9.81
layer_block = 4


def extended_2(block, sides, width):
    for axis, dim in sides:
        count = lax.axis_size(axis)
        forward = [(i, i + 1) for i in range(count - 1)]
        backward = [(target, source) for source, target in forward]
        low = lax.ppermute(
            lax.slice_in_dim(block, block.shape[dim] - width, None, axis=dim), axis, forward
        )
        high = lax.ppermute(lax.slice_in_dim(block, 0, width, axis=dim), axis, backward)
        block = jnp.concatenate([low, block, high], axis=dim)
    return block


def shifted(value, axis, steps):
    count = lax.axis_size(axis)
    leading, last = (max(0, -steps), min(count, count - steps))
    return lax.ppermute(value, axis, [(source, source + steps) for source in range(leading, last)])


def occupied(cell_counts):
    filled = jnp.repeat(cell_counts, SLOTS, axis=-1)
    slot_index = jnp.arange(filled.shape[-1], dtype=jnp.int32) % SLOTS
    return (slot_index < filled).astype(jnp.float32)


def pair_rates(center, beside_all):
    span_x, span_y, span_z = (center.shape[1], center.shape[2], center.shape[3])
    dens_c = center[6] + 1.0 - center[7]
    dens_n = beside_all[6] + 1.0 - beside_all[7]
    ratio_c = eos_stiff * (dens_c**7 - 1.0) / (dens_c * dens_c)
    ratio_n = eos_stiff * (dens_n**7 - 1.0) / (dens_n * dens_n)
    accel_sum = jnp.zeros((3,) + center.shape[1:], jnp.float32)
    drift_sum = jnp.zeros(center.shape[1:], jnp.float32)
    for step_x in range(3):
        for step_y in range(3):
            for step_z in range(3):
                neighbour = beside_all[
                    :, step_x : step_x + span_x, step_y : step_y + span_y, step_z : step_z + span_z
                ]
                near_dens = dens_n[
                    step_x : step_x + span_x, step_y : step_y + span_y, step_z : step_z + span_z
                ]
                near_ratio = ratio_n[
                    step_x : step_x + span_x, step_y : step_y + span_y, step_z : step_z + span_z
                ]
                cell_gap = (
                    jnp.array(
                        [float(1 - step_x), float(1 - step_y), float(1 - step_z)], jnp.float32
                    ).reshape(3, 1, 1, 1, 1, 1)
                    * cell_side
                )
                offset_vec = center[0:3, ..., None] - neighbour[0:3, ..., None, :] + cell_gap
                dist_sq = jnp.sum(offset_vec * offset_vec, axis=0)
                support = jnp.maximum(1.0 - jnp.sqrt(dist_sq) / (2.0 * smoothing), 0.0)
                slope_term = grad_scale * support * support * support * neighbour[7][..., None, :]
                approach = jnp.sum(
                    (center[3:6, ..., None] - neighbour[3:6, ..., None, :]) * offset_vec, axis=0
                )
                mean_dens = 0.5 * (dens_c[..., None] + near_dens[..., None, :])
                visc_term = (
                    -viscosity
                    * sound_speed
                    * smoothing
                    * jnp.minimum(approach, 0.0)
                    / ((dist_sq + visc_floor) * mean_dens)
                )
                force_term = (
                    ratio_c[..., None] + near_ratio[..., None, :] + visc_term
                ) * slope_term
                accel_sum = accel_sum - particle_mass * jnp.sum(force_term * offset_vec, axis=-1)
                drift_sum = drift_sum + particle_mass * jnp.sum(slope_term * approach, axis=-1)
    gravity_vec = jnp.array([0.0, 0.0, gravity], jnp.float32).reshape(3, 1, 1, 1, 1)
    return jnp.concatenate([accel_sum - gravity_vec, drift_sum[None]], axis=0)


def region_rates(extended):
    span_x = extended.shape[1] - 2
    span_y = extended.shape[2] - 2
    layers = extended.shape[3] // SLOTS
    cells_grid = extended.reshape(8, span_x + 2, span_y + 2, layers, SLOTS)
    padded = jnp.pad(cells_grid, ((0, 0), (0, 0), (0, 0), (1, 1), (0, 0)))

    def one_block(block_index):
        layer_start = block_index * layer_block
        beside_all = lax.dynamic_slice_in_dim(padded, layer_start, layer_block + 2, axis=3)
        return pair_rates(beside_all[:, 1:-1, 1:-1, 1:-1], beside_all)

    stacked = lax.map(one_block, jnp.arange(layers // layer_block, dtype=jnp.int32))
    ordered = jnp.moveaxis(stacked, 0, 3)
    return ordered.reshape(4, span_x, span_y, layers * SLOTS)


def predict(fields, rates_now):
    position = fields[0:3] + 0.5 * time_step * fields[3:6]
    velocity = fields[3:6] + 0.5 * time_step * rates_now[0:3]
    density = fields[6:7] + 0.5 * time_step * rates_now[3:4]
    return jnp.concatenate([position, velocity, density, fields[7:8]], axis=0)


def correct(fields, rates_mid):
    velocity = fields[3:6] + time_step * rates_mid[0:3]
    density = fields[6:7] + time_step * rates_mid[3:4]
    position = fields[0:3] + 0.5 * time_step * (fields[3:6] + velocity)
    return jnp.concatenate([position, velocity, density], axis=0)


def pack_leavers(face_state, face_count, face_leave):
    cell_total = face_count.shape[0] * face_count.shape[1]
    row_total = cell_total * LMAX // 2
    leave_quota = face_leave.reshape(cell_total)
    occupancy = face_count.reshape(cell_total)
    row_ends = jnp.cumsum(leave_quota, dtype=jnp.int32)
    starts = row_ends - leave_quota
    row_ids = jnp.arange(row_total, dtype=jnp.int32)
    owner_mask = (starts[None, :] <= row_ids[:, None]) & (row_ends[None, :] > row_ids[:, None])
    root = jnp.arange(cell_total, dtype=jnp.int32) * SLOTS + occupancy - leave_quota - starts
    source_row = jnp.sum(jnp.where(owner_mask, root[None, :], 0), axis=1, dtype=jnp.int32) + row_ids
    flat_face = face_state.reshape(7, cell_total * SLOTS)
    return jnp.take(flat_face, source_row, axis=1)


def shards(particles, counts, leavers):
    size_x = particles.shape[1]
    fields = jnp.concatenate([particles, occupied(counts)[None]], axis=0)
    current = fields
    for section_no in range(2):
        rates_now = region_rates(extended_2(current, (("slab", 1), ("tile", 2)), 1))
        if section_no == 0:
            current = predict(fields, rates_now)
    updated = correct(fields, rates_now)
    remain = counts.at[0].add(-leavers[0, 0]).at[size_x - 1].add(-leavers[1, 0])
    kept = updated * occupied(remain)[None]
    lower_rows = pack_leavers(updated[:, 0], counts[0], leavers[0, 0])
    upper_rows = pack_leavers(updated[:, size_x - 1], counts[size_x - 1], leavers[1, 0])
    from_below = shifted(upper_rows, "slab", 1)
    from_above = shifted(lower_rows, "slab", -1)
    return (kept, jnp.stack([from_below, from_above], axis=0))


def solution(mesh):
    return jax.shard_map(
        shards,
        mesh=mesh,
        in_specs=(
            P(None, "slab", "tile", None),
            P("slab", "tile", None),
            P(None, "slab", "tile", None),
        ),
        out_specs=(P(None, "slab", "tile", None), P(None, None, ("slab", "tile"))),
        check_vma=False,
    )
```

profile of v0, /device:TPU:9, one launch (start us, length us, event | category | flops | bytes accessed | tf_op | source)
XLA Modules:
  0.0 1138.1 jit_solution(14106067027984600465)
XLA Ops:
  13.9 4.0 collective-permute-start.2
  20.5 4.4 collective-permute-done.3
  33.4 525.1 %while.30 = (s32[]{:T(128)}, f32[12,4,2,2,4,32]{5,4,3,2,1,0:T(4,128)}, s32[12]{0:T(128)}, f32[8,4,4,50,32]{4,3,0,2,1:T(8,128)}, s32[]{:T(128)}, /*index=5*/f32[3...) while((s32[]{:T(128)}, ...), condition=%wide.region_109.110_spmd.clone, body=%wide.region_0.109_spmd.sunk.clone.sunk | while | flops 21704204 | bytes 16404091 | solution.py:113
  35.5 5.0 constant_dynamic-slice_fusion.166
  40.6 3.7 multiply_reduce_fusion.237
  79.3 5.0 constant_dynamic-slice_fusion.166
  84.5 3.7 multiply_reduce_fusion.237
  123.2 5.0 constant_dynamic-slice_fusion.166
  128.4 3.7 multiply_reduce_fusion.237
  166.9 5.0 constant_dynamic-slice_fusion.166
  172.0 3.7 multiply_reduce_fusion.237
  210.6 4.7 constant_dynamic-slice_fusion.166
  215.4 3.7 multiply_reduce_fusion.237
  254.0 4.7 constant_dynamic-slice_fusion.166
  258.8 3.7 multiply_reduce_fusion.237
  297.4 5.0 constant_dynamic-slice_fusion.166
  302.5 3.7 multiply_reduce_fusion.237
  341.1 5.0 constant_dynamic-slice_fusion.166
  346.2 3.7 multiply_reduce_fusion.237
  384.7 5.0 constant_dynamic-slice_fusion.166
  389.8 3.7 multiply_reduce_fusion.237
  428.6 5.0 constant_dynamic-slice_fusion.166
  433.7 3.7 multiply_reduce_fusion.237
  472.5 5.1 constant_dynamic-slice_fusion.166
  477.6 3.7 multiply_reduce_fusion.237
  516.2 5.1 constant_dynamic-slice_fusion.166
  563.6 4.3 collective-permute-start.4
  570.4 3.8 collective-permute-done.5
  581.2 4.4 collective-permute-done.7
  593.2 525.1 %while.31 = (s32[]{:T(128)}, f32[12,4,2,2,4,32]{5,4,3,2,1,0:T(4,128)}, s32[12]{0:T(128)}, f32[8,4,4,50,32]{4,3,0,2,1:T(8,128)}, s32[]{:T(128)}, /*index=5*/f32[3...) while((s32[]{:T(128)}, ...), condition=%wide.region_219.220_spmd.clone, body=%wide.region_110.219_spmd.sunk.clone.sunk | while | flops 21704204 | bytes 16404091 | solution.py:113
  595.3 5.0 constant_dynamic-slice_fusion.167
  639.2 5.0 constant_dynamic-slice_fusion.167
  644.3 3.7 multiply_reduce_fusion.249
  683.1 5.0 constant_dynamic-slice_fusion.167
  688.2 3.7 multiply_reduce_fusion.249
  726.8 5.0 constant_dynamic-slice_fusion.167
  770.6 4.6 constant_dynamic-slice_fusion.167
  814.0 4.6 constant_dynamic-slice_fusion.167
  857.4 5.0 constant_dynamic-slice_fusion.167
  901.1 5.0 constant_dynamic-slice_fusion.167
  944.8 4.9 constant_dynamic-slice_fusion.167
  949.8 3.7 multiply_reduce_fusion.249
  988.7 4.9 constant_dynamic-slice_fusion.167
  993.7 3.7 multiply_reduce_fusion.249
  1032.6 5.0 constant_dynamic-slice_fusion.167
  1076.4 5.0 constant_dynamic-slice_fusion.167
  1125.4 4.5 collective-permute-start.8
  1132.7 4.4 collective-permute-done.9
  (5775 shorter events, 875.9 us)
Async XLA Ops:
  1.5 24.8 %copy-start.112 = (f32[1,2,2,1536]{3,2,1,0:T(2,128)}, f32[1,2,2,1536]{3,2,1,0:T(2,128)S(1)}, u32[]{:S(2)}) copy-start(f32[1,2,2,1536]{3,2,1,0:T(2,128)S(1)} %compare_convert_fusion.1) | copy-start | bytes 73732
  2.6 9.9 collective-permute-start
  5.7 6.8 collective-permute-start.1
  11.3 15.1 %copy-start.210 = (s32[192]{0:T(256)}, s32[192]{0:T(256)S(1)}, u32[]{:S(2)}) copy-start(s32[192]{0:T(256)S(1)} %select_reduce_fusion) | copy-start | bytes 2308
  13.9 6.6 collective-permute-start.2
  17.9 7.0 collective-permute-start.3
  35.4 8.9 copy-start.160
  35.4 8.9 copy-start.166
  35.4 8.9 copy-start.172
  35.4 8.9 copy-start.176
  79.3 8.9 copy-start.160
  79.3 8.9 copy-start.166
  79.3 8.9 copy-start.172
  297.3 8.9 copy-start.160
  297.3 8.9 copy-start.166
  297.3 8.9 copy-start.172
  341.0 8.9 copy-start.160
  341.0 8.9 copy-start.166
  341.0 8.9 copy-start.172
  472.4 9.0 copy-start.160
  472.4 9.0 copy-start.166
  472.4 9.0 copy-start.172
  472.4 9.0 copy-start.176
  472.4 9.0 copy-start.180
  516.2 9.0 copy-start.160
  516.2 9.0 copy-start.166
  516.2 9.0 copy-start.172
  516.2 9.0 copy-start.176
  516.2 9.0 copy-start.180
  558.5 22.0 %copy-start.211 = (s32[192]{0:T(256)S(1)}, s32[192]{0:T(256)}, u32[]{:S(2)}) copy-start(s32[192]{0:T(256)} %copy-done.210) | copy-start | bytes 2308
  558.5 27.1 %copy-start.113 = (f32[1,2,2,1536]{3,2,1,0:T(2,128)S(1)}, f32[1,2,2,1536]{3,2,1,0:T(2,128)}, u32[]{:S(2)}) copy-start(f32[1,2,2,1536]{3,2,1,0:T(2,128)} %copy-done.112) | copy-start | bytes 73732
  563.6 6.8 collective-permute-start.4
  567.9 6.4 collective-permute-start.5
  575.5 5.7 collective-permute-start.6
  578.6 7.0 collective-permute-start.7
  1032.5 8.9 copy-start.162
  1032.5 8.9 copy-start.168
  1032.5 8.9 copy-start.174
  1032.6 8.9 copy-start.178
  1032.6 8.9 copy-start.182
  1076.3 8.9 copy-start.162
  1076.3 8.9 copy-start.168
  1076.3 8.9 copy-start.174
  1076.4 8.9 copy-start.178
  1076.4 8.9 copy-start.182
  1118.2 13.0 %copy-start.213 = (pred[192]{0:T(512)(128)(4,1)S(1)}, pred[192]{0:T(512)(128)(4,1)}, u32[]{:S(2)}) copy-start(pred[192]{0:T(512)(128)(4,1)} %compare_and_fusion) | copy-start | bytes 580
  1125.4 7.3 collective-permute-start.8
  1131.4 5.8 collective-permute-start.9
  (2464 other events, 11981.7 us)
where the time goes:
time: 1160 us; the launch traced here: 1140 us
  other arithmetic  793 us (68%)
  local copies, waits for them, and re-layouts  243 us (21%)
  loops' own time  57 us (5%)
  starting transfers between devices  26.8 us (2%)
  waiting for transfers between devices  17.3 us (1%)
    reduce_sum x120, other arithmetic, pair_rates(): jnp.sum(force_term * offset_vec, axis=-1)  259 us
    reduce_sum x120, other arithmetic, pair_rates(): dist_sq = jnp.sum(offset_vec * offset_vec, axis=0)  225 us
    mul x168, other arithmetic, pair_rates(): (ratio_c[..., None] + near_ratio[..., None, :] + visc_term) * slope_term  177 us
    slice x24, local copies, waits for them, and re-layouts, pair_rates(): neighbour[3:6, ..., None, :]  119 us
    mul x24, local copies, waits for them, and re-layouts, pair_rates(): grad_scale * support * support * support * neighbour[7][..., None, :]  60.5 us
    another operation x2, loops' own time, region_rates(): lax.map(one_block, jnp.arange(layers // layer_block, dtype=jnp.int32))  57 us
    reduce_sum x48, other arithmetic, pair_rates(): jnp.sum(slope_term * approach, axis=-1)  43.6 us
    dynamic_slice x24, local copies, waits for them, and re-layouts, region_rates(): lax.map(one_block, jnp.arange(layers // layer_block, dtype=jnp.int32))  29.4 us

commit v1 on v0

v1 whole, which is shorter than its diff:
```python
import math

import jax
import jax.numpy as jnp
from jax import lax
from jax.experimental import pallas as pl
from jax.experimental.pallas import tpu as pltpu
from jax.sharding import PartitionSpec as P

SLOTS = 32
LMAX = 4

sound_speed = 10.0
smoothing = 0.5
kernel_norm = 21.0 / (16.0 * math.pi * smoothing**3)
grad_scale = -5.0 * kernel_norm / (smoothing * smoothing)
eos_stiff = sound_speed * sound_speed / 7.0
particle_mass = 0.125
viscosity = 0.1
visc_floor = 0.01 * smoothing * smoothing
time_step = 0.01
gravity = 9.81
visc_scale = 2.0 * viscosity * sound_speed * smoothing
far = 1.0e6
HALF = 16


def shifted(value, axis, steps):
    count = lax.axis_size(axis)
    leading, last = (max(0, -steps), min(count, count - steps))
    return lax.ppermute(value, axis, [(source, source + steps) for source in range(leading, last)])


def occupied(cell_counts):
    filled = jnp.repeat(cell_counts, SLOTS, axis=-1)
    slot_index = jnp.arange(filled.shape[-1], dtype=jnp.int32) % SLOTS
    return slot_index < filled


def packed_blocks(chunks, cy, lane, row):
    hole_group = 3 if cy == 0 else 0
    hole = (lane >= 32 * hole_group) & (lane < 32 * hole_group + 32)
    groups = (0, 1, 2) if cy == 0 else (1, 2, 3)
    blocks = []
    for n in range(6):
        group = groups[n % 3]
        moved = pltpu.roll(chunks[7 + n // 3], (32 * (hole_group - group)) % 128, 1)
        blocks.append(jnp.where(hole, moved, chunks[n]))
    blocks.append(jnp.where(hole & (row == 0), far, chunks[6]))
    return blocks


def level_rates(load, res_ref, pack_ref):
    lane = lax.broadcasted_iota(jnp.int32, (8, 128), 1)
    row = lax.broadcasted_iota(jnp.int32, (8, 128), 0)
    lane_half = lax.broadcasted_iota(jnp.int32, (HALF, 128), 1)
    for cx in range(2):
        chunks = [load(dz, cx + dx) for dz in range(3) for dx in range(3)]
        columns = jnp.transpose(load(1, cx + 1))
        for cy in range(2):
            cell = 2 * cx + cy
            blocks = packed_blocks(chunks, cy, lane, row)
            for n in range(7):
                pack_ref[cell, n] = blocks[n]
            for half in range(SLOTS // HALF):
                first = 32 * (cy + 1) + HALF * half
                own = [
                    jnp.broadcast_to(columns[first : first + HALF, c : c + 1], (HALF, 128))
                    for c in range(8)
                ]
                total = [jnp.zeros((HALF, 128), jnp.float32) for _ in range(4)]
                for n in range(7):
                    near = [pack_ref[cell, n, c : c + 1, :] for c in range(8)]
                    rx = own[0] - near[0]
                    ry = own[1] - near[1]
                    rz = own[2] - near[2]
                    dist_sq = rx * rx + ry * ry + rz * rz
                    dist = dist_sq * lax.rsqrt(jnp.maximum(dist_sq, 1e-30))
                    support = jnp.maximum(1.0 - dist, 0.0)
                    cube = support * support * support
                    approach = (
                        (own[3] - near[3]) * rx + (own[4] - near[4]) * ry + (own[5] - near[5]) * rz
                    )
                    inverse = pl.reciprocal(
                        (dist_sq + visc_floor) * (own[6] + near[6]), approx=True
                    )
                    force = (
                        (own[7] + near[7]) - jnp.minimum(approach, 0.0) * inverse
                    ) * cube
                    total[0] = total[0] + force * rx
                    total[1] = total[1] + force * ry
                    total[2] = total[2] + force * rz
                    total[3] = total[3] + cube * approach
                sums = [jnp.sum(t, axis=1, keepdims=True) for t in total]
                merged = jnp.where(
                    lane_half < 2,
                    jnp.where(lane_half < 1, sums[0], sums[1]),
                    jnp.where(lane_half < 3, sums[2], sums[3]),
                )
                base = SLOTS * cell + HALF * half
                res_ref[base : base + HALF, :] = merged
    rates = jnp.transpose(res_ref[...])[0:8]
    scale = -particle_mass * grad_scale
    return rates * jnp.where(row < 3, scale, -scale) - jnp.where(row == 2, gravity, 0.0)


def rates_kernel(grid_ref, out_ref, res_ref, pack_ref):
    level = pl.program_id(0)
    out_ref[0] = level_rates(lambda dz, x: grid_ref[level + dz, x], res_ref, pack_ref)


def rates_call(grid):
    levels = grid.shape[0] - 2
    return pl.pallas_call(
        rates_kernel,
        grid=(levels,),
        out_shape=jax.ShapeDtypeStruct((levels, 8, 128), jnp.float32),
        in_specs=[pl.BlockSpec(grid.shape, lambda k: (0, 0, 0, 0))],
        out_specs=pl.BlockSpec((1, 8, 128), lambda k: (k, 0, 0)),
        scratch_shapes=[
            pltpu.VMEM((128, 128), jnp.float32),
            pltpu.VMEM((4, 7, 8, 128), jnp.float32),
        ],
        compiler_params=pltpu.CompilerParams(vmem_limit_bytes=32 * 1024 * 1024),
    )(grid)


def neighbourhood(own):
    levels = own.shape[0]
    low = shifted(own[:, :, :, 1:2], "tile", 1)
    high = shifted(own[:, :, :, 0:1], "tile", -1)
    wide = jnp.concatenate([low, own, high], axis=3)
    left = shifted(wide[:, :, 1:2], "slab", 1)
    right = shifted(wide[:, :, 0:1], "slab", -1)
    full = jnp.concatenate([left, wide, right], axis=2)
    full = jnp.pad(full, ((1, 1), (0, 0), (0, 0), (0, 0), (0, 0)))
    occ = full[:, 7] > 0.5
    at_x = lax.broadcasted_iota(jnp.int32, occ.shape, 1).astype(jnp.float32)
    at_y = lax.broadcasted_iota(jnp.int32, occ.shape, 2).astype(jnp.float32)
    at_z = lax.broadcasted_iota(jnp.int32, occ.shape, 0).astype(jnp.float32)
    dens = jnp.where(occ, full[:, 6], 1.0)
    dens_2 = dens * dens
    ratio = eos_stiff * (dens_2 * dens_2 * dens_2 * dens - 1.0) / dens_2
    rows = [
        jnp.where(occ, full[:, 0] + at_x, far),
        full[:, 1] + at_y,
        full[:, 2] + at_z,
        full[:, 3],
        full[:, 4],
        full[:, 5],
        dens / visc_scale,
        ratio,
    ]
    rows = jnp.stack([r.reshape(levels + 2, 4, 128) for r in rows], axis=2)
    return rows


def pack_leavers(face_state, face_count, face_leave):
    cell_total = face_count.shape[0] * face_count.shape[1]
    row_total = cell_total * LMAX // 2
    leave_quota = face_leave.reshape(cell_total)
    occupancy = face_count.reshape(cell_total)
    row_ends = jnp.cumsum(leave_quota, dtype=jnp.int32)
    starts = row_ends - leave_quota
    row_ids = jnp.arange(row_total, dtype=jnp.int32)
    owner_mask = (starts[None, :] <= row_ids[:, None]) & (row_ends[None, :] > row_ids[:, None])
    root = jnp.arange(cell_total, dtype=jnp.int32) * SLOTS + occupancy - leave_quota - starts
    source_row = jnp.sum(jnp.where(owner_mask, root[None, :], 0), axis=1, dtype=jnp.int32) + row_ids
    flat_face = face_state.reshape(7, cell_total * SLOTS)
    return jnp.take(flat_face, source_row, axis=1)


def shards(particles, counts, leavers):
    levels = counts.shape[2]
    occ = occupied(counts)
    clean = jnp.where(occ[None], particles, 0.0)
    fields = jnp.concatenate([clean, occ.astype(jnp.float32)[None]], axis=0)
    own = jnp.transpose(fields.reshape(8, 2, 2, levels, SLOTS), (3, 0, 1, 2, 4))
    rates_now = rates_call(neighbourhood(own)).reshape(levels, 8, 2, 2, SLOTS)
    half = 0.5 * time_step
    moved = jnp.concatenate(
        [
            own[:, 0:3] + half * own[:, 3:6],
            own[:, 3:7] + half * rates_now[:, 0:4],
            own[:, 7:8],
        ],
        axis=1,
    )
    rates_mid = rates_call(neighbourhood(moved)).reshape(levels, 8, 2, 2, SLOTS)
    later = own[:, 3:7] + time_step * rates_mid[:, 0:4]
    place = own[:, 0:3] + half * (own[:, 3:6] + later[:, 0:3])
    updated = jnp.concatenate([place, later], axis=1)
    updated = jnp.transpose(updated, (1, 2, 3, 0, 4)).reshape(7, 2, 2, levels * SLOTS)
    remain = counts.at[0].add(-leavers[0, 0]).at[1].add(-leavers[1, 0])
    kept = jnp.where(occupied(remain)[None], updated, 0.0)
    lower_rows = pack_leavers(updated[:, 0], counts[0], leavers[0, 0])
    upper_rows = pack_leavers(updated[:, 1], counts[1], leavers[1, 0])
    from_below = shifted(upper_rows, "slab", 1)
    from_above = shifted(lower_rows, "slab", -1)
    return (kept, jnp.stack([from_below, from_above], axis=0))


def solution(mesh):
    return jax.shard_map(
        shards,
        mesh=mesh,
        in_specs=(
            P(None, "slab", "tile", None),
            P("slab", "tile", None),
            P(None, "slab", "tile", None),
        ),
        out_specs=(P(None, "slab", "tile", None), P(None, None, ("slab", "tile"))),
        check_vma=False,
    )
```

time: 1160 us -> 231 us (0.20); the launches traced: 1140 us -> 231 us
  other arithmetic: 793 us -> 7.87 us
  local copies, waits for them, and re-layouts: 243 us -> 12.9 us
  Pallas kernels: 0 us -> 129 us
  loops' own time: 57 us -> 0 us
  waiting for transfers between devices: 17.3 us -> 57.6 us
    reduce_sum x288 -> x0, other arithmetic: 528 us -> none  [the longest x120 259 us: pair_rates(): jnp.sum(force_term * offset_vec, axis=-1)]
    mul x173 -> x0, other arithmetic: 182 us -> none  [the longest x168 177 us: pair_rates(): (ratio_c[..., None] + near_ratio[..., None, :] + visc_term) * slope_term]
    pallas_call x0 -> x2, Pallas kernels: none -> 129 us  [rates_call(): pl.pallas_call(rates_kernel, grid=(levels,), out_shape=jax.ShapeDtypeStru...]
    slice x102 -> x10, local copies, waits for them, and re-layouts: 122 us -> 1.06 us  [the longest x2 0.51 us: shards(): upper_rows = pack_leavers(updated[:, 1], counts[1], leavers[1, 0])]
    mul x32 -> x0, local copies, waits for them, and re-layouts: 61.4 us -> none  [the longest x24 60.5 us: pair_rates(): grad_scale * support * support * support * neighbour[7][..., None, :]]
    another operation x2 -> x0, loops' own time: 57 us -> none  [region_rates(): lax.map(one_block, jnp.arange(layers // layer_block, dtype=jnp.int32))]
    ppermute x2 -> x10, waiting for transfers between devices: 4.43 us -> 57.6 us  [shifted(): lax.ppermute(value, axis, [(source, source + steps) for source in range(l...]
    div x48 -> x2, other arithmetic: 47.1 us -> 0.79 us  [neighbourhood(): ratio = eos_stiff * (dens_2 * dens_2 * dens_2 * dens - 1.0) / dens_2]
where the time goes in v1:
time: 231 us
  Pallas kernels  129 us (56%)
  waiting for transfers between devices  57.6 us (25%)
  starting transfers between devices  22.2 us (10%)
  local copies, waits for them, and re-layouts  12.9 us (6%)
  other arithmetic  7.87 us (3%)
    pallas_call x2, Pallas kernels, rates_call(): pl.pallas_call(rates_kernel, grid=(levels,), out_shape=jax.ShapeDtypeStru...  129 us
    ppermute x10, waiting for transfers between devices, shifted(): lax.ppermute(value, axis, [(source, source + steps) for source in range(l...  57.6 us
    ppermute x10, starting transfers between devices, shifted(): lax.ppermute(value, axis, [(source, source + steps) for source in range(l...  22.2 us
  transfers between devices with their start and end apart: 10, of which 8 were waited for; matrix products, arithmetic and copies ran while one was open for 2% of the time, Pallas kernels for 0%

profile of v1, /device:TPU:9, one launch (start us, length us, event | category | flops | bytes accessed | tf_op | source)
XLA Modules:
  0.0 231.0 jit_solution(264401916716405407)
XLA Ops:
  0.6 0.7 copy.197
  1.5 0.7 fusion.24
  2.2 0.7 fusion.15
  3.2 1.0 broadcast_select_fusion
  4.2 0.3 concatenate.28
  4.5 0.2 copy.162
  4.8 3.8 %collective-permute-start = (f32[48,8,2,1,32]{0,4,3,2,1:T(8,128)S(1)}, f32[48,8,2,1,32]{0,4,3,2,1:T(8,128)S(1)}, u32[]{:S(2)}, u32[]{:S(2)}) collective-permute-start(f32[48,8,2,1,32]{0,4,3,2,1:T(8,128)S(1)} %get-tuple-element.59), channel_id=1, source_target_pairs={{0,1},{1,2},{2,3},{3,4},{4,5},{5,6},{6,7},{8,9},{9,10},{10,11},{11... | collective-permute-start | bytes 294920 | tf_op jit(solution)/shard_map/ppermute | solution.py:31
  8.6 1.9 collective-permute-start.1
  12.2 4.1 %collective-permute-done.1 = f32[48,8,2,1,32]{0,4,3,2,1:T(8,128)S(1)} collective-permute-done((f32[48,8,2,1,32]{0,4,3,2,1:T(8,128)S(1)}, f32[48,8,2,1,32]{0,4,3,2,1:T(8,128)S(1)}, u32[]{:S(2)}, u32[]{:S(2)}) %collective-permute-start.1) | collective-permute-done | bytes 98336 | tf_op jit(solution)/shard_map/ppermute | solution.py:31
  16.5 3.1 %collective-permute-start.2 = (f32[48,8,1,4,32]{0,4,3,2,1:T(8,128)S(1)}, f32[48,8,1,4,32]{0,4,3,2,1:T(8,128)S(1)}, u32[]{:S(2)}, u32[]{:S(2)}) collective-permute-start(f32[48,8,1,4,32]{0,4,3,2,1:T(8,128)S(1)} %get-tuple-element.55), channel_id=1, source_target_pairs={{0,8},{8,16},{16,24},{1,9},{9,17},{17,25},{2,10},{10,18},{18,26},{... | collective-permute-start | bytes 589832 | tf_op jit(solution)/shard_map/ppermute | solution.py:31
  19.7 1.3 collective-permute-start.3
  21.0 9.5 %collective-permute-done.2 = f32[48,8,1,4,32]{0,4,3,2,1:T(8,128)S(1)} collective-permute-done((f32[48,8,1,4,32]{0,4,3,2,1:T(8,128)S(1)}, f32[48,8,1,4,32]{0,4,3,2,1:T(8,128)S(1)}, u32[]{:S(2)}, u32[]{:S(2)}) %collective-permute-start.2) | collective-permute-done | bytes 196640 | tf_op jit(solution)/shard_map/ppermute | solution.py:31
  30.5 12.9 %collective-permute-done.3 = f32[48,8,1,4,32]{0,4,3,2,1:T(8,128)S(1)} collective-permute-done((f32[48,8,1,4,32]{0,4,3,2,1:T(8,128)S(1)}, f32[48,8,1,4,32]{0,4,3,2,1:T(8,128)S(1)}, u32[]{:S(2)}, u32[]{:S(2)}) %collective-permute-start.3) | collective-permute-done | bytes 196640 | tf_op jit(solution)/shard_map/ppermute | solution.py:31
  43.4 0.6 select_maximum_fusion.6
  44.0 0.1 fusion.18
  44.5 0.4 copy.164
  45.1 0.1 copy.171
  45.3 0.1 copy.172
  45.9 0.4 multiply_divide_fusion.1
  46.3 1.8 stack.15.grid_ref
  48.1 64.6 %shard_map.50 = f32[48,8,128]{2,1,0:T(8,128)S(1)} custom-call(f32[50,4,8,128]{3,2,1,0:T(8,128)S(1)} %stack.15.grid_ref), custom_call_target="tpu_custom_call" | custom-call | tf_op jit(solution)/shard_map/pallas_call | solution.py:114
  112.8 0.2 copy.174
  113.2 2.9 %collective-permute-start.4 = (f32[48,8,2,1,32]{0,4,3,2,1:T(8,128)S(1)}, f32[48,8,2,1,32]{0,4,3,2,1:T(8,128)S(1)}, u32[]{:S(2)}, u32[]{:S(2)}) collective-permute-start(f32[48,8,2,1,32]{0,4,3,2,1:T(8,128)S(1)} %get-tuple-element.57), channel_id=1, source_target_pairs={{0,1},{1,2},{2,3},{3,4},{4,5},{5,6},{6,7},{8,9},{9,10},{10,11},{11... | collective-permute-start | bytes 294920 | tf_op jit(solution)/shard_map/ppermute | solution.py:31
  116.1 1.9 collective-permute-start.5
  118.0 1.4 collective-permute-done.4
  119.4 4.4 %collective-permute-done.5 = f32[48,8,2,1,32]{0,4,3,2,1:T(8,128)S(1)} collective-permute-done((f32[48,8,2,1,32]{0,4,3,2,1:T(8,128)S(1)}, f32[48,8,2,1,32]{0,4,3,2,1:T(8,128)S(1)}, u32[]{:S(2)}, u32[]{:S(2)}) %collective-permute-start.5) | collective-permute-done | bytes 98336 | tf_op jit(solution)/shard_map/ppermute | solution.py:31
  124.0 3.1 %collective-permute-start.6 = (f32[48,8,1,4,32]{0,4,3,2,1:T(8,128)S(1)}, f32[48,8,1,4,32]{0,4,3,2,1:T(8,128)S(1)}, u32[]{:S(2)}, u32[]{:S(2)}) collective-permute-start(f32[48,8,1,4,32]{0,4,3,2,1:T(8,128)S(1)} %get-tuple-element.53), channel_id=1, source_target_pairs={{0,8},{8,16},{16,24},{1,9},{9,17},{17,25},{2,10},{10,18},{18,26},{... | collective-permute-start | bytes 589832 | tf_op jit(solution)/shard_map/ppermute | solution.py:31
  127.1 1.3 collective-permute-start.7
  128.5 9.5 %collective-permute-done.6 = f32[48,8,1,4,32]{0,4,3,2,1:T(8,128)S(1)} collective-permute-done((f32[48,8,1,4,32]{0,4,3,2,1:T(8,128)S(1)}, f32[48,8,1,4,32]{0,4,3,2,1:T(8,128)S(1)}, u32[]{:S(2)}, u32[]{:S(2)}) %collective-permute-start.6) | collective-permute-done | bytes 196640 | tf_op jit(solution)/shard_map/ppermute | solution.py:31
  138.0 11.4 %collective-permute-done.7 = f32[48,8,1,4,32]{0,4,3,2,1:T(8,128)S(1)} collective-permute-done((f32[48,8,1,4,32]{0,4,3,2,1:T(8,128)S(1)}, f32[48,8,1,4,32]{0,4,3,2,1:T(8,128)S(1)}, u32[]{:S(2)}, u32[]{:S(2)}) %collective-permute-start.7) | collective-permute-done | bytes 196640 | tf_op jit(solution)/shard_map/ppermute | solution.py:31
  149.4 0.6 select_maximum_fusion
  150.0 0.1 fusion.17
  150.5 0.4 copy.176
  151.8 0.4 multiply_divide_fusion
  152.2 1.8 stack.16.grid_ref
  154.0 64.6 %shard_map.51 = f32[48,8,128]{2,1,0:T(8,128)S(1)} custom-call(f32[50,4,8,128]{3,2,1,0:T(8,128)S(1)} %stack.16.grid_ref), custom_call_target="tpu_custom_call" | custom-call | tf_op jit(solution)/shard_map/pallas_call | solution.py:114
  218.6 0.2 copy.186
  219.0 0.3 copy.187
  219.3 0.3 reshape.407
  219.7 0.5 copy.189
  220.2 0.7 gather_fusion
  221.0 1.5 collective-permute-start.8
  222.4 0.5 copy.191
  222.9 0.7 gather_fusion.1
  223.7 1.3 collective-permute-start.9
  225.0 0.8 broadcast_select_fusion.1
  225.9 4.5 %collective-permute-done.9 = f32[7,192]{0,1:T(8,128)S(1)} collective-permute-done((f32[7,192]{0,1:T(8,128)S(1)}, f32[7,192]{0,1:T(8,128)S(1)}, u32[]{:S(2)}, u32[]{:S(2)}) %collective-permute-start.9) | collective-permute-done | bytes 5408 | tf_op jit(solution)/shard_map/ppermute | solution.py:31
  230.4 0.6 pad_maximum_fusion.3
  (76 shorter events, 5.4 us)
Async XLA Ops:
  4.5 6.1 %copy-start = (s32[2,1,2,48]{3,2,1,0:T(2,128)S(1)}, s32[2,1,2,48]{3,2,1,0:T(2,128)}, u32[]{:S(2)}) copy-start(s32[2,1,2,48]{3,2,1,0:T(2,128)} %param.11) | copy-start | bytes 2308
  4.8 7.3 %collective-permute-start = (f32[48,8,2,1,32]{0,4,3,2,1:T(8,128)S(1)}, f32[48,8,2,1,32]{0,4,3,2,1:T(8,128)S(1)}, u32[]{:S(2)}, u32[]{:S(2)}) collective-permute-start(f32[48,8,2,1,32]{0,4,3,2,1:T(8,128)S(1)} %get-tuple-element.59), channel_id=1, source_target_pairs={{0,1},{1,2},{2,3},{3,4},{4,5},{5,6},{6,7},{8,9},{9,10},{10,11},{11... | collective-permute-start | bytes 294920 | tf_op jit(solution)/shard_map/ppermute | solution.py:31
  8.6 7.7 %collective-permute-start.1 = (f32[48,8,2,1,32]{0,4,3,2,1:T(8,128)S(1)}, f32[48,8,2,1,32]{0,4,3,2,1:T(8,128)S(1)}, u32[]{:S(2)}, u32[]{:S(2)}) collective-permute-start(f32[48,8,2,1,32]{0,4,3,2,1:T(8,128)S(1)} %get-tuple-element.60), channel_id=1, source_target_pairs={{1,0},{2,1},{3,2},{4,3},{5,4},{6,5},{7,6},{9,8},{10,9},{11,10},{12... | collective-permute-start | bytes 294920 | tf_op jit(solution)/shard_map/ppermute | solution.py:31
  16.5 14.0 %collective-permute-start.2 = (f32[48,8,1,4,32]{0,4,3,2,1:T(8,128)S(1)}, f32[48,8,1,4,32]{0,4,3,2,1:T(8,128)S(1)}, u32[]{:S(2)}, u32[]{:S(2)}) collective-permute-start(f32[48,8,1,4,32]{0,4,3,2,1:T(8,128)S(1)} %get-tuple-element.55), channel_id=1, source_target_pairs={{0,8},{8,16},{16,24},{1,9},{9,17},{17,25},{2,10},{10,18},{18,26},{... | collective-permute-start | bytes 589832 | tf_op jit(solution)/shard_map/ppermute | solution.py:31
  19.7 23.7 %collective-permute-start.3 = (f32[48,8,1,4,32]{0,4,3,2,1:T(8,128)S(1)}, f32[48,8,1,4,32]{0,4,3,2,1:T(8,128)S(1)}, u32[]{:S(2)}, u32[]{:S(2)}) collective-permute-start(f32[48,8,1,4,32]{0,4,3,2,1:T(8,128)S(1)} %get-tuple-element.56), channel_id=1, source_target_pairs={{8,0},{16,8},{24,16},{9,1},{17,9},{25,17},{10,2},{18,10},{26,18},{... | collective-permute-start | bytes 589832 | tf_op jit(solution)/shard_map/ppermute | solution.py:31
  113.2 6.2 %collective-permute-start.4 = (f32[48,8,2,1,32]{0,4,3,2,1:T(8,128)S(1)}, f32[48,8,2,1,32]{0,4,3,2,1:T(8,128)S(1)}, u32[]{:S(2)}, u32[]{:S(2)}) collective-permute-start(f32[48,8,2,1,32]{0,4,3,2,1:T(8,128)S(1)} %get-tuple-element.57), channel_id=1, source_target_pairs={{0,1},{1,2},{2,3},{3,4},{4,5},{5,6},{6,7},{8,9},{9,10},{10,11},{11... | collective-permute-start | bytes 294920 | tf_op jit(solution)/shard_map/ppermute | solution.py:31
  116.1 7.7 %collective-permute-start.5 = (f32[48,8,2,1,32]{0,4,3,2,1:T(8,128)S(1)}, f32[48,8,2,1,32]{0,4,3,2,1:T(8,128)S(1)}, u32[]{:S(2)}, u32[]{:S(2)}) collective-permute-start(f32[48,8,2,1,32]{0,4,3,2,1:T(8,128)S(1)} %get-tuple-element.58), channel_id=1, source_target_pairs={{1,0},{2,1},{3,2},{4,3},{5,4},{6,5},{7,6},{9,8},{10,9},{11,10},{12... | collective-permute-start | bytes 294920 | tf_op jit(solution)/shard_map/ppermute | solution.py:31
  124.0 14.0 %collective-permute-start.6 = (f32[48,8,1,4,32]{0,4,3,2,1:T(8,128)S(1)}, f32[48,8,1,4,32]{0,4,3,2,1:T(8,128)S(1)}, u32[]{:S(2)}, u32[]{:S(2)}) collective-permute-start(f32[48,8,1,4,32]{0,4,3,2,1:T(8,128)S(1)} %get-tuple-element.53), channel_id=1, source_target_pairs={{0,8},{8,16},{16,24},{1,9},{9,17},{17,25},{2,10},{10,18},{18,26},{... | collective-permute-start | bytes 589832 | tf_op jit(solution)/shard_map/ppermute | solution.py:31
  127.1 22.2 %collective-permute-start.7 = (f32[48,8,1,4,32]{0,4,3,2,1:T(8,128)S(1)}, f32[48,8,1,4,32]{0,4,3,2,1:T(8,128)S(1)}, u32[]{:S(2)}, u32[]{:S(2)}) collective-permute-start(f32[48,8,1,4,32]{0,4,3,2,1:T(8,128)S(1)} %get-tuple-element.54), channel_id=1, source_target_pairs={{8,0},{16,8},{24,16},{9,1},{17,9},{25,17},{10,2},{18,10},{26,18},{... | collective-permute-start | bytes 589832 | tf_op jit(solution)/shard_map/ppermute | solution.py:31
  221.0 4.8 %collective-permute-start.8 = (f32[7,192]{0,1:T(8,128)S(1)}, f32[7,192]{0,1:T(8,128)S(1)}, u32[]{:S(2)}, u32[]{:S(2)}) collective-permute-start(f32[7,192]{0,1:T(8,128)S(1)} %select_bitcast_fusion.1), channel_id=1, source_target_pairs={{0,8},{8,16},{16,24},{1,9},{9,17},{17,25},{2,10},{10,18},{18,26},{... | collective-permute-start | bytes 16136 | tf_op jit(solution)/shard_map/ppermute | solution.py:31
  223.7 6.6 %collective-permute-start.9 = (f32[7,192]{0,1:T(8,128)S(1)}, f32[7,192]{0,1:T(8,128)S(1)}, u32[]{:S(2)}, u32[]{:S(2)}) collective-permute-start(f32[7,192]{0,1:T(8,128)S(1)} %select_bitcast_fusion), channel_id=1, source_target_pairs={{8,0},{16,8},{24,16},{9,1},{17,9},{25,17},{10,2},{18,10},{26,18},{... | collective-permute-start | bytes 16136 | tf_op jit(solution)/shard_map/ppermute | solution.py:31

commit v2 on v1

v2 whole, which is shorter than its diff:
```python
import math

import jax
import jax.numpy as jnp
import numpy as np
from jax import lax
from jax.experimental import pallas as pl
from jax.experimental.pallas import tpu as pltpu
from jax.sharding import PartitionSpec as P

SLOTS = 32
LMAX = 4

sound_speed = 10.0
smoothing = 0.5
kernel_norm = 21.0 / (16.0 * math.pi * smoothing**3)
grad_scale = -5.0 * kernel_norm / (smoothing * smoothing)
eos_stiff = sound_speed * sound_speed / 7.0
particle_mass = 0.125
viscosity = 0.1
visc_floor = 0.01 * smoothing * smoothing
time_step = 0.01
gravity = 9.81
visc_scale = 2.0 * viscosity * sound_speed * smoothing
far = 1.0e6


def shifted(value, axis, steps):
    count = lax.axis_size(axis)
    leading, last = (max(0, -steps), min(count, count - steps))
    return lax.ppermute(value, axis, [(source, source + steps) for source in range(leading, last)])


def occupied(cell_counts):
    filled = jnp.repeat(cell_counts, SLOTS, axis=-1)
    slot_index = jnp.arange(filled.shape[-1], dtype=jnp.int32) % SLOTS
    return slot_index < filled


def selector():
    lane = np.arange(128)
    at_x, at_y = lane // 64, lane // SLOTS % 2
    chosen = np.zeros((3, 16, 9, 128), np.float32)
    for dx in range(3):
        for dy in range(3):
            chosen[:, 4 * (at_x + dx) + at_y + dy, 3 * dx + dy, lane] = 1.0
    return chosen.reshape(48, 9 * 128)


def exchange_kernel(own_ref, out_ref, send_sem, recv_sem, local_sem):
    slab, tile = lax.axis_index("slab"), lax.axis_index("tile")
    slabs, tiles = lax.axis_size("slab"), lax.axis_size("tile")
    barrier = pltpu.get_barrier_semaphore()
    sides = [(a, b) for a in (-1, 0, 1) for b in (-1, 0, 1) if (a, b) != (0, 0)]

    def present(a, b):
        return (
            (slab + a >= 0) & (slab + a < slabs) & (tile + b >= 0) & (tile + b < tiles)
        )

    def copy(n):
        a, b = sides[n]
        source = {-1: pl.ds(0, 1), 0: pl.ds(0, 2), 1: pl.ds(1, 1)}
        target = {-1: pl.ds(3, 1), 0: pl.ds(1, 2), 1: pl.ds(0, 1)}
        return pltpu.make_async_remote_copy(
            src_ref=own_ref.at[source[a], source[b]],
            dst_ref=out_ref.at[target[a], target[b]],
            send_sem=send_sem.at[n],
            recv_sem=recv_sem.at[n],
            device_id=(slab + a, tile + b),
            device_id_type=pl.DeviceIdType.MESH,
        )

    def arrival(n):
        a, b = sides[n]
        source = {-1: pl.ds(0, 1), 0: pl.ds(0, 2), 1: pl.ds(1, 1)}
        target = {-1: pl.ds(3, 1), 0: pl.ds(1, 2), 1: pl.ds(0, 1)}
        return pltpu.make_async_remote_copy(
            src_ref=own_ref.at[source[a], source[b]],
            dst_ref=out_ref.at[target[a], target[b]],
            send_sem=send_sem.at[n],
            recv_sem=recv_sem.at[n],
            device_id=(slab, tile),
            device_id_type=pl.DeviceIdType.MESH,
        )

    count = 0
    for a, b in sides:
        there = present(a, b)
        count = count + there.astype(jnp.int32)

        @pl.when(there)
        def _():
            pl.semaphore_signal(
                barrier,
                inc=1,
                device_id=(slab + a, tile + b),
                device_id_type=pl.DeviceIdType.MESH,
            )

    local = pltpu.make_async_copy(own_ref, out_ref.at[pl.ds(1, 2), pl.ds(1, 2)], local_sem)
    local.start()
    pl.semaphore_wait(barrier, count)
    for n, (a, b) in enumerate(sides):

        @pl.when(present(a, b))
        def _():
            copy(n).start()

    local.wait()
    for n, (a, b) in enumerate(sides):

        @pl.when(present(a, b))
        def _():
            copy(n).wait_send()

        @pl.when(present(-a, -b))
        def _():
            arrival(n).wait_recv()


def exchange(own, number):
    return pl.pallas_call(
        exchange_kernel,
        out_shape=jax.ShapeDtypeStruct((4, 4) + own.shape[2:], jnp.float32),
        in_specs=[pl.BlockSpec(memory_space=pl.ANY)],
        out_specs=pl.BlockSpec(memory_space=pl.ANY),
        scratch_shapes=[
            pltpu.SemaphoreType.DMA((8,)),
            pltpu.SemaphoreType.DMA((8,)),
            pltpu.SemaphoreType.DMA,
        ],
        compiler_params=pltpu.CompilerParams(collective_id=number, has_side_effects=True),
    )(own)


def spread(raw, select):
    lane = lax.broadcasted_iota(jnp.int32, (16, 128), 1)
    column = lax.broadcasted_iota(jnp.int32, (16, 128), 0)
    low, high = raw[:, :128], raw[:, 128:]
    after = pltpu.roll(high, 32, 1)
    before = pltpu.roll(high, 96, 1)
    at_x = ((column // 4) - 1).astype(jnp.float32)
    at_y = ((column % 4) - 1).astype(jnp.float32)
    offset = jnp.where(lane < 32, at_x, jnp.where(lane < 64, at_y, 0.0))
    low = jnp.where((lane < 32) & (after < 0.5), far, low + offset)
    dens = jnp.where(before > 0.5, high, 1.0)
    dens_n = jnp.where(high > 0.5, after, 1.0)
    dens_2 = dens_n * dens_n
    ratio = eos_stiff * (dens_2 * dens_2 * dens_2 * dens_n - 1.0) / dens_2
    high = jnp.where(lane < 64, high, jnp.where(lane < 96, dens * (1.0 / visc_scale), ratio))
    value = jnp.concatenate([low, high], axis=1)
    first = value.astype(jnp.bfloat16).astype(jnp.float32)
    rest = value - first
    second = rest.astype(jnp.bfloat16).astype(jnp.float32)
    third = rest - second
    parts = jnp.transpose(jnp.concatenate([first, second, third], axis=0)).astype(jnp.bfloat16)
    return jnp.dot(parts, select, preferred_element_type=jnp.float32)


def pair_level(levels, slot_mask):
    own = []
    for c in range(8):
        value = levels[1][SLOTS * c : SLOTS * (c + 1), 4 * 128 : 5 * 128]
        own.append(jnp.sum(jnp.where(slot_mask, value, 0.0), axis=0, keepdims=True))
    own = [jnp.broadcast_to(o, (8, 128)) for o in own]
    total = [jnp.zeros((8, 128), jnp.float32) for _ in range(4)]
    for dz in range(3):
        own_z = own[2] + float(1 - dz)
        for d in range(9):
            for j in range(0, SLOTS, 8):
                near = [
                    levels[dz][SLOTS * c + j : SLOTS * c + j + 8, 128 * d : 128 * d + 128]
                    for c in range(8)
                ]
                rx = own[0] - near[0]
                ry = own[1] - near[1]
                rz = own_z - near[2]
                dist_sq = rx * rx + ry * ry + rz * rz
                dist = dist_sq * lax.rsqrt(jnp.maximum(dist_sq, 1e-30))
                support = jnp.maximum(1.0 - dist, 0.0)
                cube = support * support * support
                approach = (
                    (own[3] - near[3]) * rx + (own[4] - near[4]) * ry + (own[5] - near[5]) * rz
                )
                inverse = pl.reciprocal((dist_sq + visc_floor) * (own[6] + near[6]), approx=True)
                force = ((own[7] + near[7]) - jnp.minimum(approach, 0.0) * inverse) * cube
                total[0] = total[0] + force * rx
                total[1] = total[1] + force * ry
                total[2] = total[2] + force * rz
                total[3] = total[3] + cube * approach
    sums = [jnp.sum(t, axis=0, keepdims=True) for t in total]
    row = lax.broadcasted_iota(jnp.int32, (8, 128), 0)
    rates = jnp.where(
        row < 2,
        jnp.where(row < 1, sums[0], sums[1]),
        jnp.where(row < 3, sums[2], sums[3]),
    )
    scale = -particle_mass * grad_scale
    return rates * jnp.where(row < 3, scale, -scale) - jnp.where(row == 2, gravity, 0.0)


def rates_kernel(columns_ref, here_ref, select_ref, out_ref, *spread_refs):
    step = pl.program_id(0)
    count = columns_ref.shape[2]

    def build(level, target):
        at = jnp.clip(level, 0, count - 1)
        raw = jnp.concatenate(
            [columns_ref[x, y, pl.ds(at, 1), :] for x in range(4) for y in range(4)], axis=0
        )
        inside = jnp.where((level >= 0) & (level < count), 1.0, 0.0)
        target[...] = spread(
            jnp.where(here_ref[...] * inside > 0.5, raw, 0.0), select_ref[...]
        )

    @pl.when(step == 0)
    def _():
        build(jnp.int32(-1), spread_refs[0])
        build(jnp.int32(0), spread_refs[1])

    lane = lax.broadcasted_iota(jnp.int32, (SLOTS, 128), 1)
    slot = lax.broadcasted_iota(jnp.int32, (SLOTS, 128), 0)
    slot_mask = lane % SLOTS == slot
    for n in range(4):
        build(step * 4 + n + 1, spread_refs[(n + 2) % 4])
        out_ref[n] = pair_level([spread_refs[(n + i) % 4] for i in range(3)], slot_mask)


def rates_call(columns, here):
    levels = columns.shape[2]
    select = jnp.asarray(selector(), jnp.bfloat16)
    return pl.pallas_call(
        rates_kernel,
        grid=(levels // 4,),
        out_shape=jax.ShapeDtypeStruct((levels, 8, 128), jnp.float32),
        in_specs=[
            pl.BlockSpec(columns.shape, lambda k: (0, 0, 0, 0)),
            pl.BlockSpec(here.shape, lambda k: (0, 0)),
            pl.BlockSpec(select.shape, lambda k: (0, 0)),
        ],
        out_specs=pl.BlockSpec((4, 8, 128), lambda k: (k, 0, 0)),
        scratch_shapes=[pltpu.VMEM((8 * SLOTS, 9 * 128), jnp.float32) for _ in range(4)],
        compiler_params=pltpu.CompilerParams(vmem_limit_bytes=40 * 1024 * 1024),
    )(columns, here, select)


def by_column(rates):
    levels = rates.shape[0]
    return jnp.transpose(rates.reshape(levels, 8, 2, 2, SLOTS)[:, 0:4], (2, 3, 0, 1, 4))


def existing():
    slab, tile = lax.axis_index("slab"), lax.axis_index("tile")
    column = lax.broadcasted_iota(jnp.int32, (16, 256), 0)
    at_x = 2 * slab - 1 + column // 4
    at_y = 2 * tile - 1 + column % 4
    inside = (at_x >= 0) & (at_x < 2 * lax.axis_size("slab"))
    inside = inside & (at_y >= 0) & (at_y < 2 * lax.axis_size("tile"))
    return inside.astype(jnp.float32)


def pack_leavers(face_state, face_count, face_leave):
    cell_total = face_count.shape[0] * face_count.shape[1]
    row_total = cell_total * LMAX // 2
    leave_quota = face_leave.reshape(cell_total)
    occupancy = face_count.reshape(cell_total)
    row_ends = jnp.cumsum(leave_quota, dtype=jnp.int32)
    starts = row_ends - leave_quota
    row_ids = jnp.arange(row_total, dtype=jnp.int32)
    owner_mask = (starts[None, :] <= row_ids[:, None]) & (row_ends[None, :] > row_ids[:, None])
    root = jnp.arange(cell_total, dtype=jnp.int32) * SLOTS + occupancy - leave_quota - starts
    source_row = jnp.sum(jnp.where(owner_mask, root[None, :], 0), axis=1, dtype=jnp.int32) + row_ids
    flat_face = face_state.reshape(7, cell_total * SLOTS)
    return jnp.take(flat_face, source_row, axis=1)


def shards(particles, counts, leavers):
    levels = counts.shape[2]
    occ = occupied(counts)
    clean = jnp.where(occ[None], particles, 0.0)
    fields = jnp.concatenate([clean, occ.astype(jnp.float32)[None]], axis=0)
    own = jnp.transpose(fields.reshape(8, 2, 2, levels, SLOTS), (1, 2, 3, 0, 4))
    here = existing()
    half = 0.5 * time_step
    block = (2, 2, levels, 8 * SLOTS)
    rates_now = by_column(rates_call(exchange(own.reshape(block), 0), here))
    moved = jnp.concatenate(
        [
            own[..., 0:3, :] + half * own[..., 3:6, :],
            own[..., 3:7, :] + half * rates_now,
            own[..., 7:8, :],
        ],
        axis=3,
    )
    moved = jnp.where(own[..., 7:8, :] > 0.5, moved, 0.0)
    rates_mid = by_column(rates_call(exchange(moved.reshape(block), 1), here))
    later = own[..., 3:7, :] + time_step * rates_mid
    place = own[..., 0:3, :] + half * (own[..., 3:6, :] + later[..., 0:3, :])
    updated = jnp.concatenate([place, later], axis=3)
    updated = jnp.transpose(updated, (3, 0, 1, 2, 4)).reshape(7, 2, 2, levels * SLOTS)
    remain = counts.at[0].add(-leavers[0, 0]).at[1].add(-leavers[1, 0])
    kept = jnp.where(occupied(remain)[None], updated, 0.0)
    lower_rows = pack_leavers(updated[:, 0], counts[0], leavers[0, 0])
    upper_rows = pack_leavers(updated[:, 1], counts[1], leavers[1, 0])
    from_below = shifted(upper_rows, "slab", 1)
    from_above = shifted(lower_rows, "slab", -1)
    return (kept, jnp.stack([from_below, from_above], axis=0))


def solution(mesh):
    return jax.shard_map(
        shards,
        mesh=mesh,
        in_specs=(
            P(None, "slab", "tile", None),
            P("slab", "tile", None),
            P(None, "slab", "tile", None),
        ),
        out_specs=(P(None, "slab", "tile", None), P(None, None, ("slab", "tile"))),
        check_vma=False,
    )
```

time: 231 us -> 129 us (0.56)
  waiting for transfers between devices: 57.6 us -> 5.81 us
  Pallas kernels: 129 us -> 98.6 us
  starting transfers between devices: 22.2 us -> 5.86 us
  other arithmetic: 7.87 us -> 5.41 us
    ppermute x10 -> x2, waiting for transfers between devices: 57.6 us -> 5.81 us  [shifted(): lax.ppermute(value, axis, [(source, source + steps) for source in range(l...]
    pallas_call x2 -> x4, Pallas kernels: 129 us -> 98.6 us  [the longest x2 76 us: rates_call(): pl.pallas_call(rates_kernel, grid=(levels // 4,), out_shape=jax.ShapeDtyp...]
    ppermute x10 -> x2, starting transfers between devices: 22.2 us -> 5.86 us  [shifted(): lax.ppermute(value, axis, [(source, source + steps) for source in range(l...]
    another operation x10 -> x2, local copies, waits for them, and re-layouts: 4.65 us -> 0.22 us  [the longest x8 4.42 us: neighbourhood(): rows = jnp.stack([r.reshape(levels + 2, 4, 128) for r in rows], axis=2)]
    unnamed x3 -> x11, local copies, waits for them, and re-layouts: 0.69 us -> 3.4 us
  transfers between devices with their start and end apart: 10 -> 2, of which waited for: 8 -> 1; matrix products, arithmetic and copies ran while one was open for 2% -> 2% of each run, Pallas kernels for 0% -> 0%
where the time goes in v2:
time: 129 us; the launch traced here: 127 us
  Pallas kernels  98.6 us (76%)
  local copies, waits for them, and re-layouts  10.7 us (8%)
  starting transfers between devices  5.86 us (5%)
  waiting for transfers between devices  5.81 us (5%)
  other arithmetic  5.41 us (4%)
    pallas_call x2, Pallas kernels, rates_call(): pl.pallas_call(rates_kernel, grid=(levels // 4,), out_shape=jax.ShapeDtyp...  76 us
    pallas_call x2, Pallas kernels, exchange(): pl.pallas_call(exchange_kernel, out_shape=jax.ShapeDtypeStruct((4, 4) + o...  22.7 us
    ppermute x2, starting transfers between devices, shifted(): lax.ppermute(value, axis, [(source, source + steps) for source in range(l...  5.86 us
    ppermute x2, waiting for transfers between devices, shifted(): lax.ppermute(value, axis, [(source, source + steps) for source in range(l...  5.81 us
    unnamed x11, local copies, waits for them, and re-layouts  3.4 us
  transfers between devices with their start and end apart: 2, of which 1 were waited for; matrix products, arithmetic and copies ran while one was open for 2% of the time, Pallas kernels for 0%

profile of v2, /device:TPU:9, one launch (start us, length us, event | category | flops | bytes accessed | tf_op | source)
XLA Modules:
  0.0 127.5 jit_solution(14580859501731786316)
XLA Ops:
  0.6 0.7 copy.57
  1.4 0.1 compare_convert_fusion
  1.6 0.1 reshape.234
  1.7 0.7 fusion.21
  2.4 0.7 fusion.18
  3.1 0.1 broadcast_in_dim.82
  3.2 0.1 reshape.233
  3.3 1.0 broadcast_select_fusion
  4.3 0.3 concatenate.16
  4.7 0.5 copy.40
  5.3 0.1 copy-done.3
  5.4 0.1 reshape.265
  5.5 0.1 reshape_squeeze.19
  5.7 0.1 reduce-window.14
  5.8 0.1 reduce.4
  5.9 0.1 select_reduce_fusion.1
  6.1 0.9 reshape.235.own_ref
  7.0 10.6 %shard_map.68.columns_ref = f32[4,4,48,256]{3,2,1,0:T(8,128)} custom-call(f32[2,2,48,256]{3,2,1,0:T(8,128)} %reshape.235.own_ref), custom_call_target="tpu_custom_call" | custom-call | tf_op jit(solution)/shard_map/pallas_call | solution.py:123
  17.6 0.1 fusion.14.here_ref
  17.7 1.1 copy-done
  18.8 37.9 %shard_map.69 = f32[48,8,128]{2,1,0:T(8,128)S(1)} custom-call(f32[4,4,48,256]{3,2,1,0:T(8,128)S(1)} %copy-done, f32[16,256]{1,0:T(8,128)S(1)} %fusion.14.here_ref, bf16[48,1152]{1,0:T(8,128)(2,1)S(1)} %copy-done.2), custom_call_target="tpu_custom_call" | custom-call | tf_op jit(solution)/shard_map/pallas_call | solution.py:233
  56.8 0.2 copy.41
  57.0 0.2 copy.52
  57.3 0.1 maximum_select_fusion
  57.3 0.5 copy.43
  57.8 0.9 select_n.64.own_ref
  58.7 12.1 %shard_map.70.columns_ref = f32[4,4,48,256]{3,2,1,0:T(8,128)} custom-call(f32[2,2,48,256]{3,2,1,0:T(8,128)} %select_n.64.own_ref), custom_call_target="tpu_custom_call" | custom-call | tf_op jit(solution)/shard_map/pallas_call | solution.py:123
  70.8 1.1 copy-done.1
  72.0 38.0 %shard_map.71 = f32[48,8,128]{2,1,0:T(8,128)S(1)} custom-call(f32[4,4,48,256]{3,2,1,0:T(8,128)S(1)} %copy-done.1, f32[16,256]{1,0:T(8,128)S(1)} %fusion.14.here_ref, bf16[48,1152]{1,0:T(8,128)(2,1)S(1)} %copy-done.2), custom_call_target="tpu_custom_call" | custom-call | tf_op jit(solution)/shard_map/pallas_call | solution.py:233
  110.0 0.2 copy.44
  110.2 0.2 copy.53
  110.6 0.3 reshape.238
  111.0 0.5 copy.47
  111.5 0.7 gather_fusion
  112.2 0.1 select_bitcast_fusion.1
  112.3 4.6 %collective-permute-start = (f32[7,192]{0,1:T(8,128)S(1)}, f32[7,192]{0,1:T(8,128)S(1)}, u32[]{:S(2)}, u32[]{:S(2)}) collective-permute-start(f32[7,192]{0,1:T(8,128)S(1)} %select_bitcast_fusion.1), channel_id=1, source_target_pairs={{0,8},{8,16},{16,24},{1,9},{9,17},{17,25},{2,10},{10,18},{18,26},{... | collective-permute-start | bytes 16136 | tf_op jit(solution)/shard_map/ppermute | solution.py:31
  116.8 0.1 reshape.266
  117.0 0.1 reshape_squeeze.22
  117.1 0.1 reduce-window.15
  117.3 0.1 reduce.5
  117.4 0.1 select_reduce_fusion
  117.5 0.5 copy.49
  118.0 0.7 gather_fusion.1
  118.7 0.1 select_bitcast_fusion
  118.8 1.3 %collective-permute-start.1 = (f32[7,192]{0,1:T(8,128)S(1)}, f32[7,192]{0,1:T(8,128)S(1)}, u32[]{:S(2)}, u32[]{:S(2)}) collective-permute-start(f32[7,192]{0,1:T(8,128)S(1)} %select_bitcast_fusion), channel_id=1, source_target_pairs={{8,0},{16,8},{24,16},{9,1},{17,9},{25,17},{10,2},{18,10},{26,18},{... | collective-permute-start | bytes 16136 | tf_op jit(solution)/shard_map/ppermute | solution.py:31
  120.1 0.8 broadcast_select_fusion.1
  121.0 5.8 %collective-permute-done.1 = f32[7,192]{0,1:T(8,128)S(1)} collective-permute-done((f32[7,192]{0,1:T(8,128)S(1)}, f32[7,192]{0,1:T(8,128)S(1)}, u32[]{:S(2)}, u32[]{:S(2)}) %collective-permute-start.1) | collective-permute-done | bytes 5408 | tf_op jit(solution)/shard_map/ppermute | solution.py:31
  126.9 0.6 pad_maximum_fusion
  (37 shorter events, 0.9 us)
Async XLA Ops:
  4.7 0.7 copy-start.3
  5.2 12.5 %copy-start.2 = (bf16[48,1152]{1,0:T(8,128)(2,1)S(1)}, bf16[48,1152]{1,0:T(8,128)(2,1)}, u32[]{:S(2)}) copy-start(bf16[48,1152]{1,0:T(8,128)(2,1)} %constant.149.clone.select_ref) | copy-start | bytes 331780
  17.7 1.1 copy-start
  70.8 1.1 copy-start.1
  112.3 8.6 %collective-permute-start = (f32[7,192]{0,1:T(8,128)S(1)}, f32[7,192]{0,1:T(8,128)S(1)}, u32[]{:S(2)}, u32[]{:S(2)}) collective-permute-start(f32[7,192]{0,1:T(8,128)S(1)} %select_bitcast_fusion.1), channel_id=1, source_target_pairs={{0,8},{8,16},{16,24},{1,9},{9,17},{17,25},{2,10},{10,18},{18,26},{... | collective-permute-start | bytes 16136 | tf_op jit(solution)/shard_map/ppermute | solution.py:31
  118.8 7.9 %collective-permute-start.1 = (f32[7,192]{0,1:T(8,128)S(1)}, f32[7,192]{0,1:T(8,128)S(1)}, u32[]{:S(2)}, u32[]{:S(2)}) collective-permute-start(f32[7,192]{0,1:T(8,128)S(1)} %select_bitcast_fusion), channel_id=1, source_target_pairs={{8,0},{16,8},{24,16},{9,1},{17,9},{25,17},{10,2},{18,10},{26,18},{... | collective-permute-start | bytes 16136 | tf_op jit(solution)/shard_map/ppermute | solution.py:31

commit v3 on v2

--- a/solution.py
+++ b/solution.py
@@ -1,3 +1,4 @@
+import functools
 import math
 
 import jax
@@ -25,12 +26,6 @@
 far = 1.0e6
 
 
-def shifted(value, axis, steps):
-    count = lax.axis_size(axis)
-    leading, last = (max(0, -steps), min(count, count - steps))
-    return lax.ppermute(value, axis, [(source, source + steps) for source in range(leading, last)])
-
-
 def occupied(cell_counts):
     filled = jnp.repeat(cell_counts, SLOTS, axis=-1)
     slot_index = jnp.arange(filled.shape[-1], dtype=jnp.int32) % SLOTS
@@ -58,7 +53,7 @@
             (slab + a >= 0) & (slab + a < slabs) & (tile + b >= 0) & (tile + b < tiles)
         )
 
-    def copy(n):
+    def copy(n, move=1):
         a, b = sides[n]
         source = {-1: pl.ds(0, 1), 0: pl.ds(0, 2), 1: pl.ds(1, 1)}
         target = {-1: pl.ds(3, 1), 0: pl.ds(1, 2), 1: pl.ds(0, 1)}
@@ -67,20 +62,7 @@
             dst_ref=out_ref.at[target[a], target[b]],
             send_sem=send_sem.at[n],
             recv_sem=recv_sem.at[n],
-            device_id=(slab + a, tile + b),
-            device_id_type=pl.DeviceIdType.MESH,
-        )
-
-    def arrival(n):
-        a, b = sides[n]
-        source = {-1: pl.ds(0, 1), 0: pl.ds(0, 2), 1: pl.ds(1, 1)}
-        target = {-1: pl.ds(3, 1), 0: pl.ds(1, 2), 1: pl.ds(0, 1)}
-        return pltpu.make_async_remote_copy(
-            src_ref=own_ref.at[source[a], source[b]],
-            dst_ref=out_ref.at[target[a], target[b]],
-            send_sem=send_sem.at[n],
-            recv_sem=recv_sem.at[n],
-            device_id=(slab, tile),
+            device_id=(slab + a * move, tile + b * move),
             device_id_type=pl.DeviceIdType.MESH,
         )
 
@@ -116,7 +98,7 @@
 
         @pl.when(present(-a, -b))
         def _():
-            arrival(n).wait_recv()
+            copy(n, 0).wait_recv()
 
 
 def exchange(own, number):
@@ -134,31 +116,88 @@
     )(own)
 
 
-def spread(raw, select):
+def migrate_kernel(rows_ref, out_ref, send_sem, recv_sem):
+    slab, tile = lax.axis_index("slab"), lax.axis_index("tile")
+    has_next, has_last = slab + 1 < lax.axis_size("slab"), slab > 0
+    barrier = pltpu.get_barrier_semaphore()
+
+    def copy(source, step):
+        return pltpu.make_async_remote_copy(
+            src_ref=rows_ref.at[source],
+            dst_ref=out_ref.at[1 - source],
+            send_sem=send_sem.at[source],
+            recv_sem=recv_sem.at[source],
+            device_id=(slab + step, tile),
+            device_id_type=pl.DeviceIdType.MESH,
+        )
+
+    plan = ((1, 1, has_next, has_last), (0, -1, has_last, has_next))
+    for source, step, sends, receives in plan:
+
+        @pl.when(sends)
+        def _():
+            pl.semaphore_signal(
+                barrier,
+                inc=1,
+                device_id=(slab + step, tile),
+                device_id_type=pl.DeviceIdType.MESH,
+            )
+
+    pl.semaphore_wait(barrier, has_next.astype(jnp.int32) + has_last.astype(jnp.int32))
+    for source, step, sends, receives in plan:
+
+        @pl.when(sends)
+        def _():
+            copy(source, step).start()
+
+        @pl.when(jnp.logical_not(receives))
+        def _():
+            out_ref[1 - source] = jnp.zeros(out_ref.shape[1:], jnp.float32)
+
+    for source, step, sends, receives in plan:
+
+        @pl.when(sends)
+        def _():
+            copy(source, step).wait_send()
+
+        @pl.when(receives)
+        def _():
+            copy(source, 0).wait_recv()
+
+
+def migrate(rows, number):
+    return pl.pallas_call(
+        migrate_kernel,
+        out_shape=jax.ShapeDtypeStruct(rows.shape, jnp.float32),
+        in_specs=[pl.BlockSpec(memory_space=pltpu.VMEM)],
+        out_specs=pl.BlockSpec(memory_space=pltpu.VMEM),
+        scratch_shapes=[pltpu.SemaphoreType.DMA((2,)), pltpu.SemaphoreType.DMA((2,))],
+        compiler_params=pltpu.CompilerParams(collective_id=number, has_side_effects=True),
+    )(rows)
+
+
+def column_parts(low, high):
     lane = lax.broadcasted_iota(jnp.int32, (16, 128), 1)
     column = lax.broadcasted_iota(jnp.int32, (16, 128), 0)
-    low, high = raw[:, :128], raw[:, 128:]
-    after = pltpu.roll(high, 32, 1)
-    before = pltpu.roll(high, 96, 1)
+    occ = pltpu.roll(low, 32, 1)
     at_x = ((column // 4) - 1).astype(jnp.float32)
     at_y = ((column % 4) - 1).astype(jnp.float32)
     offset = jnp.where(lane < 32, at_x, jnp.where(lane < 64, at_y, 0.0))
-    low = jnp.where((lane < 32) & (after < 0.5), far, low + offset)
-    dens = jnp.where(before > 0.5, high, 1.0)
-    dens_n = jnp.where(high > 0.5, after, 1.0)
-    dens_2 = dens_n * dens_n
-    ratio = eos_stiff * (dens_2 * dens_2 * dens_2 * dens_n - 1.0) / dens_2
-    high = jnp.where(lane < 64, high, jnp.where(lane < 96, dens * (1.0 / visc_scale), ratio))
+    dens = jnp.where(low > 0.5, high, 1.0)
+    dens_2 = dens * dens
+    ratio = eos_stiff * (dens_2 * dens_2 * dens_2 * dens - 1.0) / dens_2
+    low = jnp.where((lane < 32) & (occ < 0.5), far, low + offset)
+    low = jnp.where(lane < 96, low, ratio)
+    high = jnp.where(lane < 96, high, dens * (1.0 / visc_scale))
     value = jnp.concatenate([low, high], axis=1)
     first = value.astype(jnp.bfloat16).astype(jnp.float32)
     rest = value - first
     second = rest.astype(jnp.bfloat16).astype(jnp.float32)
     third = rest - second
-    parts = jnp.transpose(jnp.concatenate([first, second, third], axis=0)).astype(jnp.bfloat16)
-    return jnp.dot(parts, select, preferred_element_type=jnp.float32)
-
-
-def pair_level(levels, slot_mask):
+    return jnp.transpose(jnp.concatenate([first, second, third], axis=0)).astype(jnp.bfloat16)
+
+
+def pair_level(levels, slot_mask, between):
     own = []
     for c in range(8):
         value = levels[1][SLOTS * c : SLOTS * (c + 1), 4 * 128 : 5 * 128]
@@ -168,6 +207,7 @@
     for dz in range(3):
         own_z = own[2] + float(1 - dz)
         for d in range(9):
+            between(9 * dz + d)
             for j in range(0, SLOTS, 8):
                 near = [
                     levels[dz][SLOTS * c + j : SLOTS * c + j + 8, 128 * d : 128 * d + 128]
@@ -181,10 +221,10 @@
                 support = jnp.maximum(1.0 - dist, 0.0)
                 cube = support * support * support
                 approach = (
-                    (own[3] - near[3]) * rx + (own[4] - near[4]) * ry + (own[5] - near[5]) * rz
+                    (own[4] - near[4]) * rx + (own[5] - near[5]) * ry + (own[6] - near[6]) * rz
                 )
-                inverse = pl.reciprocal((dist_sq + visc_floor) * (own[6] + near[6]), approx=True)
-                force = ((own[7] + near[7]) - jnp.minimum(approach, 0.0) * inverse) * cube
+                inverse = pl.reciprocal((dist_sq + visc_floor) * (own[7] + near[7]), approx=True)
+                force = ((own[3] + near[3]) - jnp.minimum(approach, 0.0) * inverse) * cube
                 total[0] = total[0] + force * rx
                 total[1] = total[1] + force * ry
                 total[2] = total[2] + force * rz
@@ -200,49 +240,77 @@
     return rates * jnp.where(row < 3, scale, -scale) - jnp.where(row == 2, gravity, 0.0)
 
 
-def rates_kernel(columns_ref, here_ref, select_ref, out_ref, *spread_refs):
+def rates_kernel(later, *refs):
+    columns_ref = refs[0]
+    later_ref = refs[1] if later else None
+    here_ref, select_ref, out_ref, *scratch = refs[1 + later :]
+    parts_refs, spread_refs = scratch[:2], scratch[2:]
     step = pl.program_id(0)
     count = columns_ref.shape[2]
 
-    def build(level, target):
+    def prepare(level, parts_ref):
         at = jnp.clip(level, 0, count - 1)
-        raw = jnp.concatenate(
-            [columns_ref[x, y, pl.ds(at, 1), :] for x in range(4) for y in range(4)], axis=0
-        )
+
+        def rows(ref):
+            return jnp.concatenate(
+                [ref[x, y, pl.ds(at, 1), :] for x in range(4) for y in range(4)], axis=0
+            )
+
         inside = jnp.where((level >= 0) & (level < count), 1.0, 0.0)
-        target[...] = spread(
-            jnp.where(here_ref[...] * inside > 0.5, raw, 0.0), select_ref[...]
+        valid = here_ref[...] * inside > 0.5
+        raw = jnp.where(valid, rows(columns_ref), 0.0)
+        low, high = raw[:, :128], raw[:, 128:]
+        if later:
+            lane = lax.broadcasted_iota(jnp.int32, (16, 128), 1)
+            low = low + 0.5 * time_step * jnp.where(lane < 96, high, 0.0)
+            high = jnp.where(valid[:, :128], rows(later_ref), 0.0)
+        parts_ref[...] = column_parts(low, high)
+
+    def fill(n, parts_ref, target):
+        tile = slice(256 * n, min(256 * n + 256, 9 * 128))
+        target[:, tile] = jnp.dot(
+            parts_ref[...], select_ref[:, tile], preferred_element_type=jnp.float32
         )
 
     @pl.when(step == 0)
     def _():
-        build(jnp.int32(-1), spread_refs[0])
-        build(jnp.int32(0), spread_refs[1])
+        for n in range(3):
+            prepare(jnp.int32(n - 1), parts_refs[0])
+            for tile in range(5):
+                fill(tile, parts_refs[0], spread_refs[n])
 
     lane = lax.broadcasted_iota(jnp.int32, (SLOTS, 128), 1)
     slot = lax.broadcasted_iota(jnp.int32, (SLOTS, 128), 0)
     slot_mask = lane % SLOTS == slot
     for n in range(4):
-        build(step * 4 + n + 1, spread_refs[(n + 2) % 4])
-        out_ref[n] = pair_level([spread_refs[(n + i) % 4] for i in range(3)], slot_mask)
-
-
-def rates_call(columns, here):
+
+        def between(place):
+            if place == 0:
+                prepare(step * 4 + n + 2, parts_refs[n % 2])
+            elif place % 5 == 4:
+                fill(place // 5, parts_refs[n % 2], spread_refs[(n + 3) % 4])
+
+        out_ref[n] = pair_level([spread_refs[(n + i) % 4] for i in range(3)], slot_mask, between)
+
+
+def rates_call(columns, here, later=None):
     levels = columns.shape[2]
     select = jnp.asarray(selector(), jnp.bfloat16)
+    arrays = [columns] + ([] if later is None else [later])
     return pl.pallas_call(
-        rates_kernel,
+        functools.partial(rates_kernel, later is not None),
         grid=(levels // 4,),
         out_shape=jax.ShapeDtypeStruct((levels, 8, 128), jnp.float32),
-        in_specs=[
-            pl.BlockSpec(columns.shape, lambda k: (0, 0, 0, 0)),
+        in_specs=[pl.BlockSpec(a.shape, lambda k: (0, 0, 0, 0)) for a in arrays]
+        + [
             pl.BlockSpec(here.shape, lambda k: (0, 0)),
             pl.BlockSpec(select.shape, lambda k: (0, 0)),
         ],
         out_specs=pl.BlockSpec((4, 8, 128), lambda k: (k, 0, 0)),
-        scratch_shapes=[pltpu.VMEM((8 * SLOTS, 9 * 128), jnp.float32) for _ in range(4)],
+        scratch_shapes=[pltpu.VMEM((8 * SLOTS, 48), jnp.bfloat16) for _ in range(2)]
+        + [pltpu.VMEM((8 * SLOTS, 9 * 128), jnp.float32) for _ in range(4)],
         compiler_params=pltpu.CompilerParams(vmem_limit_bytes=40 * 1024 * 1024),
-    )(columns, here, select)
+    )(*arrays, here, select)
 
 
 def by_column(rates):
@@ -279,33 +347,23 @@
     levels = counts.shape[2]
     occ = occupied(counts)
     clean = jnp.where(occ[None], particles, 0.0)
-    fields = jnp.concatenate([clean, occ.astype(jnp.float32)[None]], axis=0)
+    fields = jnp.concatenate([clean[0:3], occ.astype(jnp.float32)[None], clean[3:7]], axis=0)
     own = jnp.transpose(fields.reshape(8, 2, 2, levels, SLOTS), (1, 2, 3, 0, 4))
     here = existing()
     half = 0.5 * time_step
-    block = (2, 2, levels, 8 * SLOTS)
-    rates_now = by_column(rates_call(exchange(own.reshape(block), 0), here))
-    moved = jnp.concatenate(
-        [
-            own[..., 0:3, :] + half * own[..., 3:6, :],
-            own[..., 3:7, :] + half * rates_now,
-            own[..., 7:8, :],
-        ],
-        axis=3,
-    )
-    moved = jnp.where(own[..., 7:8, :] > 0.5, moved, 0.0)
-    rates_mid = by_column(rates_call(exchange(moved.reshape(block), 1), here))
-    later = own[..., 3:7, :] + time_step * rates_mid
-    place = own[..., 0:3, :] + half * (own[..., 3:6, :] + later[..., 0:3, :])
-    updated = jnp.concatenate([place, later], axis=3)
+    columns = exchange(own.reshape(2, 2, levels, 8 * SLOTS), 0)
+    rates_now = by_column(rates_call(columns, here))
+    moved = jnp.where(own[..., 3:4, :] > 0.5, own[..., 4:8, :] + half * rates_now, 0.0)
+    later = exchange(moved.reshape(2, 2, levels, 4 * SLOTS), 1)
+    rates_mid = by_column(rates_call(columns, here, later))
+    speed = own[..., 4:8, :] + time_step * rates_mid
+    place = own[..., 0:3, :] + half * (own[..., 4:7, :] + speed[..., 0:3, :])
+    updated = jnp.concatenate([place, speed], axis=3)
     updated = jnp.transpose(updated, (3, 0, 1, 2, 4)).reshape(7, 2, 2, levels * SLOTS)
     remain = counts.at[0].add(-leavers[0, 0]).at[1].add(-leavers[1, 0])
     kept = jnp.where(occupied(remain)[None], updated, 0.0)
-    lower_rows = pack_leavers(updated[:, 0], counts[0], leavers[0, 0])
-    upper_rows = pack_leavers(updated[:, 1], counts[1], leavers[1, 0])
-    from_below = shifted(upper_rows, "slab", 1)
-    from_above = shifted(lower_rows, "slab", -1)
-    return (kept, jnp.stack([from_below, from_above], axis=0))
+    rows = jnp.stack([pack_leavers(updated[:, f], counts[f], leavers[f, 0]) for f in range(2)])
+    return (kept, migrate(rows, 2))
 
 
 def solution(mesh):

time: 129 us -> 122 us (0.946)
  starting transfers between devices: 5.86 us -> 0 us
  waiting for transfers between devices: 5.81 us -> 0 us
  Pallas kernels: 98.6 us -> 103 us
    pallas_call x2 -> x3, Pallas kernels: 76 us -> 83 us  [the longest x2 76.8 us: rates_call(): pl.pallas_call(functools.partial(rates_kernel, later is not None), grid=(...]
    ppermute x2 -> x0, starting transfers between devices: 5.86 us -> none  [shifted(): lax.ppermute(value, axis, [(source, source + steps) for source in range(l...]
    ppermute x2 -> x0, waiting for transfers between devices: 5.81 us -> none  [shifted(): lax.ppermute(value, axis, [(source, source + steps) for source in range(l...]
    pallas_call x2, Pallas kernels: 22.7 us -> 20.2 us  [exchange(): pl.pallas_call(exchange_kernel, out_shape=jax.ShapeDtypeStruct((4, 4) + o...]
    unnamed x11 -> x14, local copies, waits for them, and re-layouts: 3.4 us -> 4.49 us
  transfers between devices with their start and end apart: 2 -> 0, of which waited for: 1 -> 0; matrix products, arithmetic and copies ran while one was open for 2% -> 0% of each run, Pallas kernels for 0% -> 0%
where the time goes in v3:
time: 122 us; the launch traced here: 121 us
  Pallas kernels  103 us (84%)
  local copies, waits for them, and re-layouts  11.4 us (9%)
  other arithmetic  5.12 us (4%)
    pallas_call x2, Pallas kernels, rates_call(): pl.pallas_call(functools.partial(rates_kernel, later is not None), grid=(...  76.8 us
    pallas_call x2, Pallas kernels, exchange(): pl.pallas_call(exchange_kernel, out_shape=jax.ShapeDtypeStruct((4, 4) + o...  20.2 us
    pallas_call x1, Pallas kernels, migrate(): pl.pallas_call(migrate_kernel, out_shape=jax.ShapeDtypeStruct(rows.shape,...  6.21 us
    unnamed x14, local copies, waits for them, and re-layouts  4.49 us

profile of v3, /device:TPU:9, one launch (start us, length us, event | category | flops | bytes accessed | tf_op | source)
XLA Modules:
  0.0 120.8 jit_solution(2120109362834977734)
XLA Ops:
  0.6 0.7 copy.53
  1.3 0.1 compare_convert_fusion
  1.4 0.1 broadcast_in_dim.84
  1.5 0.7 fusion.23
  2.2 0.7 fusion.20
  2.9 0.1 broadcast_in_dim.82
  3.0 0.1 reshape.232
  3.1 0.1 reshape.233
  3.3 1.0 broadcast_select_fusion
  4.3 0.2 concatenate.16
  4.5 0.2 concatenate.15
  4.7 0.5 copy.34
  5.2 0.9 reshape.234.own_ref
  6.1 10.6 %shard_map.68.refs_0_ = f32[4,4,48,256]{3,2,1,0:T(8,128)} custom-call(f32[2,2,48,256]{3,2,1,0:T(8,128)} %reshape.234.own_ref), custom_call_target="tpu_custom_call" | custom-call | tf_op jit(solution)/shard_map/pallas_call | solution.py:105
  16.8 0.1 fusion.16.refs_1_.refs_2_
  16.9 1.1 copy-done
  18.0 38.3 %shard_map.69 = f32[48,8,128]{2,1,0:T(8,128)S(1)} custom-call(f32[4,4,48,256]{3,2,1,0:T(8,128)S(1)} %copy-done, f32[16,256]{1,0:T(8,128)S(1)} %fusion.16.refs_1_.refs_2_, bf16[48,1152]{1,0:T(8,128)(2,1)S(1)} %copy-done.3), custom_call_target="tpu_custom_call" | custom-call | tf_op jit(solution)/shard_map/pallas_call | solution.py:300
  56.3 0.2 copy.35
  56.6 0.2 copy.48
  56.9 0.2 copy.37
  57.0 0.8 copy.38.own_ref
  57.8 9.6 %shard_map.70.refs_1_ = f32[4,4,48,128]{3,2,1,0:T(8,128)} custom-call(f32[2,2,48,128]{3,2,1,0:T(8,128)} %copy.38.own_ref), custom_call_target="tpu_custom_call" | custom-call | tf_op jit(solution)/shard_map/pallas_call | solution.py:105
  67.4 1.0 copy-done.2
  68.4 38.5 %shard_map.71 = f32[48,8,128]{2,1,0:T(8,128)S(1)} custom-call(f32[4,4,48,256]{3,2,1,0:T(8,128)S(1)} %copy-done.1, f32[4,4,48,128]{3,2,1,0:T(8,128)S(1)} %copy-done.2, f32[16,256]{1,0:T(8,128)S(1)} %fusion.16.refs_1_.refs_2_, bf16[48,1152]{1,0:T(8,128)(2,1)S(1)} %copy-done.3), custom_call_target="tpu_custom_call" | custom-call | tf_op jit(solution)/shard_map/pallas_call | solution.py:300
  106.9 0.2 copy.39
  107.2 0.2 copy.49
  107.5 0.3 reshape.238
  107.9 0.5 copy.42
  108.4 0.1 reshape_squeeze.20
  108.5 0.1 reshape.265
  108.6 0.1 reduce-window.14
  108.8 0.1 reduce.4
  108.9 0.1 reshape_squeeze.19
  109.0 0.1 select_reduce_fusion.1
  109.1 0.7 gather_fusion
  109.8 0.1 copy.43
  109.9 0.5 copy.45
  110.4 0.1 reshape_squeeze.23
  110.5 0.1 reshape.266
  110.6 0.1 reduce-window.15
  110.8 0.1 reduce.5
  110.9 0.1 reshape_squeeze.22
  111.0 0.1 select_reduce_fusion
  111.1 0.7 gather_fusion.1
  111.9 0.6 pad_maximum_fusion.rows_ref
  112.5 6.2 %shard_map.72 = f32[2,7,192]{2,1,0:T(8,128)} custom-call(f32[2,7,192]{2,1,0:T(8,128)} %pad_maximum_fusion.rows_ref), custom_call_target="tpu_custom_call" | custom-call | tf_op jit(solution)/shard_map/pallas_call | solution.py:169
  118.7 1.3 %copy.47 = f32[2,7,192]{2,0,1:T(2,128)} copy(f32[2,7,192]{2,1,0:T(8,128)} %shard_map.72) | data formatting | bytes 21504
  120.1 0.8 broadcast_select_fusion.1
  (37 shorter events, 0.6 us)
Async XLA Ops:
  4.7 12.1 %copy-start.3 = (bf16[48,1152]{1,0:T(8,128)(2,1)S(1)}, bf16[48,1152]{1,0:T(8,128)(2,1)}, u32[]{:S(2)}) copy-start(bf16[48,1152]{1,0:T(8,128)(2,1)} %constant.149.clone.refs_2_.refs_3_) | copy-start | bytes 331780
  16.9 1.1 copy-start
  56.8 10.7 %copy-start.1 = (f32[4,4,48,256]{3,2,1,0:T(8,128)S(1)}, f32[4,4,48,256]{3,2,1,0:T(8,128)}, u32[]{:S(2)}) copy-start(f32[4,4,48,256]{3,2,1,0:T(8,128)} %shard_map.68.refs_0_) | copy-start | bytes 2359300
  67.4 1.0 copy-start.2
  107.5 1.0 copy-start.4

commit v4 on v3

--- a/solution.py
+++ b/solution.py
@@ -208,27 +208,22 @@
         own_z = own[2] + float(1 - dz)
         for d in range(9):
             between(9 * dz + d)
-            for j in range(0, SLOTS, 8):
-                near = [
-                    levels[dz][SLOTS * c + j : SLOTS * c + j + 8, 128 * d : 128 * d + 128]
-                    for c in range(8)
-                ]
-                rx = own[0] - near[0]
-                ry = own[1] - near[1]
-                rz = own_z - near[2]
-                dist_sq = rx * rx + ry * ry + rz * rz
-                dist = dist_sq * lax.rsqrt(jnp.maximum(dist_sq, 1e-30))
-                support = jnp.maximum(1.0 - dist, 0.0)
-                cube = support * support * support
-                approach = (
-                    (own[4] - near[4]) * rx + (own[5] - near[5]) * ry + (own[6] - near[6]) * rz
-                )
-                inverse = pl.reciprocal((dist_sq + visc_floor) * (own[7] + near[7]), approx=True)
-                force = ((own[3] + near[3]) - jnp.minimum(approach, 0.0) * inverse) * cube
-                total[0] = total[0] + force * rx
-                total[1] = total[1] + force * ry
-                total[2] = total[2] + force * rz
-                total[3] = total[3] + cube * approach
+            near = [
+                levels[dz][SLOTS * c : SLOTS * (c + 1), 128 * d : 128 * d + 128].reshape(4, 8, 128)
+                for c in range(8)
+            ]
+            rx = own[0] - near[0]
+            ry = own[1] - near[1]
+            rz = own_z - near[2]
+            dist_sq = rx * rx + ry * ry + rz * rz
+            dist = dist_sq * lax.rsqrt(jnp.maximum(dist_sq, 1e-30))
+            support = jnp.maximum(1.0 - dist, 0.0)
+            cube = support * support * support
+            approach = (own[4] - near[4]) * rx + (own[5] - near[5]) * ry + (own[6] - near[6]) * rz
+            inverse = pl.reciprocal((dist_sq + visc_floor) * (own[7] + near[7]), approx=True)
+            force = ((own[3] + near[3]) - jnp.minimum(approach, 0.0) * inverse) * cube
+            for t, term in enumerate((force * rx, force * ry, force * rz, cube * approach)):
+                total[t] = total[t] + jnp.sum(term, axis=0)
     sums = [jnp.sum(t, axis=0, keepdims=True) for t in total]
     row = lax.broadcasted_iota(jnp.int32, (8, 128), 0)
     rates = jnp.where(

time: 122 us -> 121 us (level)
    pallas_call x2, Pallas kernels: 76.8 us -> 75.5 us  [rates_call(): pl.pallas_call(functools.partial(rates_kernel, later is not None), grid=(...]
where the time goes in v4:
time: 121 us; the launch traced here: 119 us
  Pallas kernels  102 us (84%)
  local copies, waits for them, and re-layouts  11.4 us (9%)
  other arithmetic  5.12 us (4%)
    pallas_call x2, Pallas kernels, rates_call(): pl.pallas_call(functools.partial(rates_kernel, later is not None), grid=(...  75.5 us
    pallas_call x2, Pallas kernels, exchange(): pl.pallas_call(exchange_kernel, out_shape=jax.ShapeDtypeStruct((4, 4) + o...  20.2 us
    pallas_call x1, Pallas kernels, migrate(): pl.pallas_call(migrate_kernel, out_shape=jax.ShapeDtypeStruct(rows.shape,...  6.2 us
    unnamed x14, local copies, waits for them, and re-layouts  4.49 us

profile of v4, /device:TPU:9, one launch (start us, length us, event | category | flops | bytes accessed | tf_op | source)
XLA Modules:
  0.0 119.5 jit_solution(6290843436024748861)
XLA Ops:
  0.6 0.7 copy.53
  1.3 0.1 compare_convert_fusion
  1.4 0.1 broadcast_in_dim.84
  1.5 0.7 fusion.23
  2.2 0.7 fusion.20
  2.9 0.1 broadcast_in_dim.82
  3.0 0.1 reshape.232
  3.1 0.1 reshape.233
  3.3 1.0 broadcast_select_fusion
  4.3 0.2 concatenate.16
  4.5 0.2 concatenate.15
  4.7 0.5 copy.34
  5.2 0.9 reshape.234.own_ref
  6.1 10.6 %shard_map.68.refs_0_ = f32[4,4,48,256]{3,2,1,0:T(8,128)} custom-call(f32[2,2,48,256]{3,2,1,0:T(8,128)} %reshape.234.own_ref), custom_call_target="tpu_custom_call" | custom-call | tf_op jit(solution)/shard_map/pallas_call | solution.py:105
  16.8 0.1 fusion.16.refs_1_.refs_2_
  16.9 1.1 copy-done
  18.0 37.6 %shard_map.69 = f32[48,8,128]{2,1,0:T(8,128)S(1)} custom-call(f32[4,4,48,256]{3,2,1,0:T(8,128)S(1)} %copy-done, f32[16,256]{1,0:T(8,128)S(1)} %fusion.16.refs_1_.refs_2_, bf16[48,1152]{1,0:T(8,128)(2,1)S(1)} %copy-done.3), custom_call_target="tpu_custom_call" | custom-call | tf_op jit(solution)/shard_map/pallas_call | solution.py:295
  55.6 0.2 copy.35
  55.8 0.2 copy.48
  56.1 0.2 copy.37
  56.3 0.8 copy.38.own_ref
  57.0 9.6 %shard_map.70.refs_1_ = f32[4,4,48,128]{3,2,1,0:T(8,128)} custom-call(f32[2,2,48,128]{3,2,1,0:T(8,128)} %copy.38.own_ref), custom_call_target="tpu_custom_call" | custom-call | tf_op jit(solution)/shard_map/pallas_call | solution.py:105
  66.7 1.0 copy-done.2
  67.7 37.9 %shard_map.71 = f32[48,8,128]{2,1,0:T(8,128)S(1)} custom-call(f32[4,4,48,256]{3,2,1,0:T(8,128)S(1)} %copy-done.1, f32[4,4,48,128]{3,2,1,0:T(8,128)S(1)} %copy-done.2, f32[16,256]{1,0:T(8,128)S(1)} %fusion.16.refs_1_.refs_2_, bf16[48,1152]{1,0:T(8,128)(2,1)S(1)} %copy-done.3), custom_call_target="tpu_custom_call" | custom-call | tf_op jit(solution)/shard_map/pallas_call | solution.py:295
  105.6 0.2 copy.39
  105.8 0.2 copy.49
  106.2 0.3 reshape.238
  106.5 0.5 copy.42
  107.1 0.1 reshape_squeeze.20
  107.1 0.1 reshape.265
  107.3 0.1 reduce-window.14
  107.4 0.1 reduce.4
  107.5 0.1 reshape_squeeze.19
  107.6 0.1 select_reduce_fusion.1
  107.8 0.7 gather_fusion
  108.5 0.1 copy.43
  108.6 0.5 copy.45
  109.1 0.1 reshape_squeeze.23
  109.1 0.1 reshape.266
  109.3 0.1 reduce-window.15
  109.4 0.1 reduce.5
  109.5 0.1 reshape_squeeze.22
  109.6 0.1 select_reduce_fusion
  109.8 0.7 gather_fusion.1
  110.6 0.6 pad_maximum_fusion.rows_ref
  111.2 6.2 %shard_map.72 = f32[2,7,192]{2,1,0:T(8,128)} custom-call(f32[2,7,192]{2,1,0:T(8,128)} %pad_maximum_fusion.rows_ref), custom_call_target="tpu_custom_call" | custom-call | tf_op jit(solution)/shard_map/pallas_call | solution.py:169
  117.4 1.3 %copy.47 = f32[2,7,192]{2,0,1:T(2,128)} copy(f32[2,7,192]{2,1,0:T(8,128)} %shard_map.72) | data formatting | bytes 21504
  118.7 0.8 broadcast_select_fusion.1
  (37 shorter events, 0.6 us)
Async XLA Ops:
  4.7 12.1 %copy-start.3 = (bf16[48,1152]{1,0:T(8,128)(2,1)S(1)}, bf16[48,1152]{1,0:T(8,128)(2,1)}, u32[]{:S(2)}) copy-start(bf16[48,1152]{1,0:T(8,128)(2,1)} %constant.149.clone.refs_2_.refs_3_) | copy-start | bytes 331780
  16.9 1.1 copy-start
  56.0 10.7 %copy-start.1 = (f32[4,4,48,256]{3,2,1,0:T(8,128)S(1)}, f32[4,4,48,256]{3,2,1,0:T(8,128)}, u32[]{:S(2)}) copy-start(f32[4,4,48,256]{3,2,1,0:T(8,128)} %shard_map.68.refs_0_) | copy-start | bytes 2359300
  66.7 1.0 copy-start.2
  106.2 1.0 copy-start.4

commit v5 on v4

--- a/solution.py
+++ b/solution.py
@@ -46,7 +46,7 @@
     slab, tile = lax.axis_index("slab"), lax.axis_index("tile")
     slabs, tiles = lax.axis_size("slab"), lax.axis_size("tile")
     barrier = pltpu.get_barrier_semaphore()
-    sides = [(a, b) for a in (-1, 0, 1) for b in (-1, 0, 1) if (a, b) != (0, 0)]
+    sides = [(-1, 0), (1, 0), (0, -1), (0, 1), (-1, -1), (-1, 1), (1, -1), (1, 1)]
 
     def present(a, b):
         return (
@@ -56,18 +56,24 @@
     def copy(n, move=1):
         a, b = sides[n]
         source = {-1: pl.ds(0, 1), 0: pl.ds(0, 2), 1: pl.ds(1, 1)}
+        held = {-1: pl.ds(1, 1), 1: pl.ds(2, 1)}
         target = {-1: pl.ds(3, 1), 0: pl.ds(1, 2), 1: pl.ds(0, 1)}
+        corner = a != 0 and b != 0
+        if corner:
+            block, step = out_ref.at[target[a], held[b]], (0, b)
+        else:
+            block, step = own_ref.at[source[a], source[b]], (a, b)
         return pltpu.make_async_remote_copy(
-            src_ref=own_ref.at[source[a], source[b]],
+            src_ref=block,
             dst_ref=out_ref.at[target[a], target[b]],
             send_sem=send_sem.at[n],
             recv_sem=recv_sem.at[n],
-            device_id=(slab + a * move, tile + b * move),
+            device_id=(slab + step[0] * move, tile + step[1] * move),
             device_id_type=pl.DeviceIdType.MESH,
         )
 
     count = 0
-    for a, b in sides:
+    for a, b in sides[:4]:
         there = present(a, b)
         count = count + there.astype(jnp.int32)
 
@@ -83,22 +89,37 @@
     local = pltpu.make_async_copy(own_ref, out_ref.at[pl.ds(1, 2), pl.ds(1, 2)], local_sem)
     local.start()
     pl.semaphore_wait(barrier, count)
-    for n, (a, b) in enumerate(sides):
+    for n, (a, b) in enumerate(sides[:4]):
 
         @pl.when(present(a, b))
         def _():
             copy(n).start()
+
+    for n, (a, b) in enumerate(sides[:2]):
+
+        @pl.when(present(-a, 0))
+        def _():
+            copy(n, 0).wait_recv()
+
+        for m in range(4, 8):
+            if sides[m][0] == a:
+
+                @pl.when(present(-a, 0) & present(0, sides[m][1]))
+                def _():
+                    copy(m).start()
 
     local.wait()
     for n, (a, b) in enumerate(sides):
 
-        @pl.when(present(a, b))
+        @pl.when(present(a, b) if n < 4 else present(-a, 0) & present(0, b))
         def _():
             copy(n).wait_send()
 
-        @pl.when(present(-a, -b))
-        def _():
-            copy(n, 0).wait_recv()
+        if n >= 2:
+
+            @pl.when(present(-a, -b))
+            def _():
+                copy(n, 0).wait_recv()
 
 
 def exchange(own, number):

time: 121 us -> 120 us (level)
  no operation moved by 1% of the time
where the time goes in v5:
time: 120 us; the launch traced here: 119 us
  Pallas kernels  102 us (85%)
  local copies, waits for them, and re-layouts  11.4 us (10%)
  other arithmetic  5.12 us (4%)
    pallas_call x2, Pallas kernels, rates_call(): pl.pallas_call(functools.partial(rates_kernel, later is not None), grid=(...  75.5 us
    pallas_call x2, Pallas kernels, exchange(): pl.pallas_call(exchange_kernel, out_shape=jax.ShapeDtypeStruct((4, 4) + o...  20.4 us
    pallas_call x1, Pallas kernels, migrate(): pl.pallas_call(migrate_kernel, out_shape=jax.ShapeDtypeStruct(rows.shape,...  5.89 us
    unnamed x14, local copies, waits for them, and re-layouts  4.49 us

profile of v5, /device:TPU:9, one launch (start us, length us, event | category | flops | bytes accessed | tf_op | source)
XLA Modules:
  0.0 119.3 jit_solution(3993665085387135089)
XLA Ops:
  0.6 0.7 copy.53
  1.3 0.1 compare_convert_fusion
  1.4 0.1 broadcast_in_dim.84
  1.5 0.7 fusion.23
  2.2 0.7 fusion.20
  2.9 0.1 broadcast_in_dim.82
  3.0 0.1 reshape.232
  3.1 0.1 reshape.233
  3.3 1.0 broadcast_select_fusion
  4.3 0.2 concatenate.16
  4.5 0.2 concatenate.15
  4.7 0.5 copy.34
  5.2 0.9 reshape.234.own_ref
  6.1 11.0 %shard_map.68.refs_0_ = f32[4,4,48,256]{3,2,1,0:T(8,128)} custom-call(f32[2,2,48,256]{3,2,1,0:T(8,128)} %reshape.234.own_ref), custom_call_target="tpu_custom_call" | custom-call | tf_op jit(solution)/shard_map/pallas_call | solution.py:126
  17.1 0.1 fusion.16.refs_1_.refs_2_
  17.2 1.1 copy-done
  18.4 37.6 %shard_map.69 = f32[48,8,128]{2,1,0:T(8,128)S(1)} custom-call(f32[4,4,48,256]{3,2,1,0:T(8,128)S(1)} %copy-done, f32[16,256]{1,0:T(8,128)S(1)} %fusion.16.refs_1_.refs_2_, bf16[48,1152]{1,0:T(8,128)(2,1)S(1)} %copy-done.3), custom_call_target="tpu_custom_call" | custom-call | tf_op jit(solution)/shard_map/pallas_call | solution.py:316
  56.0 0.2 copy.35
  56.2 0.2 copy.48
  56.5 0.2 copy.37
  56.7 0.8 copy.38.own_ref
  57.4 9.4 %shard_map.70.refs_1_ = f32[4,4,48,128]{3,2,1,0:T(8,128)} custom-call(f32[2,2,48,128]{3,2,1,0:T(8,128)} %copy.38.own_ref), custom_call_target="tpu_custom_call" | custom-call | tf_op jit(solution)/shard_map/pallas_call | solution.py:126
  66.8 1.0 copy-done.2
  67.8 37.9 %shard_map.71 = f32[48,8,128]{2,1,0:T(8,128)S(1)} custom-call(f32[4,4,48,256]{3,2,1,0:T(8,128)S(1)} %copy-done.1, f32[4,4,48,128]{3,2,1,0:T(8,128)S(1)} %copy-done.2, f32[16,256]{1,0:T(8,128)S(1)} %fusion.16.refs_1_.refs_2_, bf16[48,1152]{1,0:T(8,128)(2,1)S(1)} %copy-done.3), custom_call_target="tpu_custom_call" | custom-call | tf_op jit(solution)/shard_map/pallas_call | solution.py:316
  105.7 0.2 copy.39
  106.0 0.2 copy.49
  106.3 0.3 reshape.238
  106.7 0.5 copy.42
  107.2 0.1 reshape_squeeze.20
  107.3 0.1 reshape.265
  107.4 0.1 reduce-window.14
  107.6 0.1 reduce.4
  107.7 0.1 reshape_squeeze.19
  107.8 0.1 select_reduce_fusion.1
  107.9 0.7 gather_fusion
  108.7 0.5 copy.45
  109.2 0.1 reshape_squeeze.23
  109.3 0.1 reshape.266
  109.4 0.1 reduce-window.15
  109.6 0.1 reduce.5
  109.7 0.1 reshape_squeeze.22
  109.8 0.1 select_reduce_fusion
  109.9 0.7 gather_fusion.1
  110.6 0.1 copy.46
  110.7 0.6 pad_maximum_fusion.rows_ref
  111.3 5.9 %shard_map.72 = f32[2,7,192]{2,1,0:T(8,128)} custom-call(f32[2,7,192]{2,1,0:T(8,128)} %pad_maximum_fusion.rows_ref), custom_call_target="tpu_custom_call" | custom-call | tf_op jit(solution)/shard_map/pallas_call | solution.py:190
  117.2 1.3 %copy.47 = f32[2,7,192]{2,0,1:T(2,128)} copy(f32[2,7,192]{2,1,0:T(8,128)} %shard_map.72) | data formatting | bytes 21504
  118.6 0.8 broadcast_select_fusion.1
  (37 shorter events, 0.6 us)
Async XLA Ops:
  4.7 12.5 %copy-start.3 = (bf16[48,1152]{1,0:T(8,128)(2,1)S(1)}, bf16[48,1152]{1,0:T(8,128)(2,1)}, u32[]{:S(2)}) copy-start(bf16[48,1152]{1,0:T(8,128)(2,1)} %constant.149.clone.refs_2_.refs_3_) | copy-start | bytes 331780
  17.2 1.1 copy-start
  56.4 10.4 %copy-start.1 = (f32[4,4,48,256]{3,2,1,0:T(8,128)S(1)}, f32[4,4,48,256]{3,2,1,0:T(8,128)}, u32[]{:S(2)}) copy-start(f32[4,4,48,256]{3,2,1,0:T(8,128)} %shard_map.68.refs_0_) | copy-start | bytes 2359300
  66.8 1.0 copy-start.2
  106.3 1.0 copy-start.4
